TPU v7x, 512 devices: a whole 4x8x8 slice. The times are simulated.
512 devices in a mesh: blk: 16 (over y_lo, x), band: 32 (over y_hi, z, core).
Axes of the slice: x: 4, y: 8 (y_hi: 2, y_lo: 4; y = y_hi * 4 + y_lo), z: 8, core: 2. Of those that a mesh axis runs over, the one named last changes fastest.
Arguments:
- fine_blocks: float32 [2048, 64, 256], P(('blk', 'band')), may hold values from -3 to 3
- source_group: int32 [2048, 4], P(('blk', 'band')), may hold values from 0 to 15, all different within a row; in each aligned block of 4 rows (0 to 3, 4 to 7, ...) at most 2 rows name the same one
- source_row: int32 [2048, 4], P(('blk', 'band')), may hold values from 0 to 3
- prolong_blocks: float32 [2048, 64, 128], P(('blk', 'band')), may hold values from -0.75 to 0.75
- prolong_code: int32 [2048, 2], P(('blk', 'band')), may hold values from 0 to 2
Outputs:
- coarse_rows: float32 [32768, 5120], P(('blk', 'band'))
Inputs may be any that keep to these rules, and one draw needn't show every extreme that they name: `source_group`: each fine block row names 4 different groups; among the rows of one device no group is named more than 2 times, and some device names one group exactly 2 times.
All inputs are finite; a program needn't handle non-finite values.
Results may differ from a plain program's by a relative error of at most 0.0003.
Values sent between devices are 32-bit elements; how exact they have to be, the bound alone decides.
A program may use at most 64 MiB of HBM per device.

v0:
```python
import jax
import jax.numpy as jnp
from jax import lax
from jax.sharding import PartitionSpec as P

CB = 1


precise = lax.Precision.HIGHEST


def with_halo(cells, sides, width):
    for axis, dim in sides:
        count = lax.axis_size(axis)
        head = lax.slice_in_dim(cells, 0, width, axis=dim)
        tail = lax.slice_in_dim(cells, cells.shape[dim] - width, cells.shape[dim], axis=dim)
        cells = jnp.concatenate(
            [
                lax.ppermute(tail, axis, [(i, (i + 1) % count) for i in range(count)]),
                cells,
                lax.ppermute(head, axis, [((i + 1) % count, i) for i in range(count)]),
            ],
            axis=dim,
        )
    return cells


def expand_codes(blocks, code_rows, slot_total):
    block_width = blocks.shape[-2]
    code_total = code_rows.shape[-1]
    shaped = blocks.reshape(blocks.shape[:-1] + (code_total, block_width))
    picker = (code_rows[..., None] == jnp.arange(slot_total, dtype=jnp.int32)).astype(jnp.float32)
    placed = jnp.einsum("...anx,...nj->...ajx", shaped, picker, precision=precise)
    return placed.reshape(blocks.shape[:-1] + (slot_total * block_width,))


def body(fine_blocks, source_group, source_row, prolong_blocks, prolong_code):
    block_width = prolong_blocks.shape[1]
    fine_rows = prolong_blocks.shape[0]
    per_row = fine_blocks.shape[2] // block_width
    slot_total = 3 * CB
    window = slot_total * block_width
    groups = lax.axis_size("blk")
    bucket_depth = min(fine_rows, 2 * fine_rows * per_row // groups)
    total_blocks = fine_rows * per_row
    blocks_flat = fine_blocks.reshape(fine_rows, block_width, per_row, block_width).transpose(
        0, 2, 1, 3
    )
    blocks_flat = blocks_flat.reshape(total_blocks, block_width, block_width)
    group_flat = source_group.reshape(total_blocks)
    row_flat = source_row.reshape(total_blocks)
    target_row = jnp.arange(total_blocks, dtype=jnp.int32) // per_row
    member = (group_flat[None, :] == jnp.arange(groups, dtype=jnp.int32)[:, None]).astype(jnp.int32)
    position = jnp.cumsum(member, axis=1) - 1
    depth_range = jnp.arange(bucket_depth, dtype=jnp.int32)
    matched = (member[:, None, :] == 1) & (position[:, None, :] == depth_range[None, :, None])
    block_range = jnp.arange(total_blocks, dtype=jnp.int32)
    bucket_block = jnp.sum(jnp.where(matched, block_range[None, None, :], 0), axis=2)
    bucket_on = jnp.any(matched, axis=2).astype(jnp.float32)
    own_window = expand_codes(prolong_blocks, prolong_code, slot_total)
    restrict = own_window.reshape(fine_rows * block_width, window)
    portion_blocks = lax.all_gather(prolong_blocks, "blk", axis=0, tiled=True)
    portion_code = lax.all_gather(prolong_code, "blk", axis=0, tiled=True)
    span_groups = portion_blocks.shape[0] // fine_rows
    local_row = (
        jnp.arange(span_groups, dtype=jnp.int32)[:, None] * fine_rows + row_flat[bucket_block]
    )
    gathered = expand_codes(portion_blocks[local_row], portion_code[local_row], slot_total)
    picked = blocks_flat[bucket_block] * bucket_on[..., None, None]
    product = jnp.einsum("qsab,qsby->qsay", picked, gathered, precision=precise)
    landing = (
        target_row[bucket_block][..., None] == jnp.arange(fine_rows, dtype=jnp.int32)
    ).astype(jnp.float32)
    applied = jnp.einsum("qsi,qsay->qiay", landing, product, precision=precise)
    applied = applied.reshape(applied.shape[0], fine_rows * block_width, window)
    collected = jnp.einsum("rj,qry->qjy", restrict, applied, precision=precise)
    coarse_height = CB * block_width
    band_width = groups * CB * block_width
    partial_value = collected.reshape(groups, 3, coarse_height, 3, CB, block_width).transpose(
        1, 2, 3, 0, 4, 5
    )
    partial_value = partial_value.reshape(3, coarse_height, 3 * band_width)
    padded = with_halo(partial_value, (("band", 0),), 1)
    lower = padded[0].reshape(coarse_height, 3, band_width)
    middle = padded[2].reshape(coarse_height, 3, band_width)
    upper = padded[4].reshape(coarse_height, 3, band_width)
    summed = jnp.pad(lower, ((0, 0), (0, 2), (0, 0))) + jnp.pad(middle, ((0, 0), (1, 1), (0, 0)))
    summed = summed + jnp.pad(upper, ((0, 0), (2, 0), (0, 0)))
    return summed.reshape(coarse_height, 5 * band_width)


def solution(mesh):
    return jax.shard_map(
        body,
        mesh=mesh,
        in_specs=(
            P(("blk", "band"), None, None),
            P(("blk", "band"), None),
            P(("blk", "band"), None),
            P(("blk", "band"), None, None),
            P(("blk", "band"), None),
        ),
        out_specs=P(("blk", "band"), None),
        check_vma=False,
    )
```

profile of v0, /device:TPU:6, one launch (start us, length us, event | category | flops | bytes accessed | tf_op | source)
XLA Modules:
  0.0 198.0 jit_solution(2311877881957650326)
XLA Ops:
  7.3 1.1 reshape.143
  8.4 0.8 eq.86
  9.1 0.8 reshape.139
  9.9 0.8 copy.63
  13.3 38.1 %all-gather = s32[16,4,2]{1,2,0:T(2,128)S(1)} all-gather(s32[1,4,2]{1,2,0:T(2,128)S(1)} %bitcast.65), channel_id=1, replica_groups=mesh['blk'=16,'band'=32] {'blk'}, dimensions={0}, use_global_device_ids=true | all-gather | bytes 544 | tf_op jit(solution)/shard_map/all_gather | solution.py:63
  51.6 0.8 convolution_bitcast_fusion.2
  52.9 1.6 gather_fusion.1
  55.0 40.0 %all-gather.3.cloned.1.call-done = f32[64,64,128]{2,1,0:T(8,128)} async-done(((f32[4,64,128]{2,1,0:T(8,128)}), f32[64,64,128]{2,1,0:T(8,128)}) %all-gather.3.cloned.1.call-update) | async-done | bytes 2097168 | tf_op jit(solution)/shard_map/all_gather | solution.py:62
  95.1 2.2 %gather_fusion.4 = f32[32,64,128]{2,1,0:T(8,128)S(1)} fusion(f32[64,64,128]{2,1,0:T(8,128)} %all-gather.3.cloned.1.call-done, s32[1024]{0:T(1024)S(1)} %pad_clamp_fusion), kind=kCustom, calls=%fused_computation.4 | custom fusion | bytes 2097280 | tf_op jit(solution)/shard_map/gather | solution.py:68
  97.3 1.2 reshape.140
  98.4 6.9 %convolution_bitcast_fusion = f32[16,2,64,3,64]{4,3,2,1,0:T(4,128)} fusion(f32[16,2,64,2,64]{4,3,2,1,0:T(2,128)S(1)} %reshape.140, s32[16,2,2]{2,1,0:T(2,128)S(1)} %bitcast.64), kind=kOutput, calls=%fused_computation.5 | convolution fusion | flops 9437376 | bytes 2621696 | tf_op jit(solution)/shard_map/...anx,...nj->...ajx/dot_general | solution.py:33
  105.3 3.4 %copy.59 = f32[16,2,64,3,64]{2,4,3,1,0:T(8,128)S(1)} copy(f32[16,2,64,3,64]{4,3,2,1,0:T(4,128)} %convolution_bitcast_fusion) | data formatting | bytes 3145728 | tf_op jit(solution)/shard_map/...anx,...nj->...ajx/transpose | solution.py:33
  108.7 7.4 %fusion.2 = f32[16,2,64,192]{3,2,1,0:T(8,128)S(1)} fusion(f32[16,2,64,192]{2,3,1,0:T(8,128)S(1)} %bitcast.59, f32[16,2,64,64]{3,2,1,0:T(8,128)} %bitcast.62, f32[16,2]{1,0:T(8,128)S(1)} %copy.52), kind=kOutput, calls=%fused_computation.11 | convolution fusion | flops 302120960 | bytes 3670144 | tf_op jit(solution)/shard_map/qsab,qsby->qsay/dot_general | solution.py:70
  116.1 6.1 %fusion = f32[16,4,64,192]{3,1,2,0:T(4,128)S(1)} fusion(f32[16,2,64,192]{3,2,1,0:T(8,128)S(1)} %fusion.2, s32[16,2]{1,0:T(8,128)S(1)} %reshape.147), kind=kOutput, calls=%fused_computation.6 | convolution fusion | flops 18874496 | bytes 4718720 | tf_op jit(solution)/shard_map/qsi,qsay->qiay/dot_general | solution.py:74
  122.9 6.7 %convolution_bitcast_fusion.1 = f32[16,192,192]{1,2,0:T(8,128)S(1)} fusion(f32[16,256,192]{2,1,0:T(8,128)S(1)} %bitcast.58, f32[256,192]{1,0:T(8,128)S(1)} %reshape.199), kind=kOutput, calls=%fused_computation.9 | convolution fusion | flops 1811939328 | bytes 5701632 | tf_op jit(solution)/shard_map/rj,qry->qjy/dot_general | solution.py:76
  129.6 2.6 %copy.66 = f32[16,192,192]{2,1,0:T(8,128)} copy(f32[16,192,192]{1,2,0:T(8,128)S(1)} %convolution_bitcast_fusion.1) | data formatting | bytes 4718592 | tf_op jit(solution)/shard_map/rj,qry->qjy/transpose | solution.py:76
  132.3 7.4 %reshape.144 = f32[16,3,64,3,1,64]{5,3,2,1,0,4:T(4,128)} reshape(f32[16,192,192]{2,1,0:T(8,128)} %copy.66) | data formatting | bytes 4718592 | tf_op jit(solution)/shard_map/reshape | solution.py:79
  139.7 5.9 %fusion.21 = (f32[1,64,3,16,1,64]{5,2,1,0,3,4:T(4,128)S(1)}, f32[1,64,3,16,1,64]{5,2,1,0,3,4:T(4,128)}, f32[1,64,3,16,1,64]{5,2,1,0,3,4:T(4,128)S(1)}) fusion(f32[3,64,3,16,1,64]{5,2,1,0,3,4:T(4,128)} %bitcast.57), kind=kLoop, calls=%fused_computation.45 | loop fusion | bytes 4718592 | tf_op jit(solution)/shard_map/slice | solution.py:16
  145.6 2.1 %copy.67 = f32[1,64,3,16,1,64]{5,3,2,1,4,0:T(8,128)} copy(f32[1,64,3,16,1,64]{5,2,1,0,3,4:T(4,128)S(1)} %get-tuple-element.5) | data formatting | bytes 1572864 | tf_op jit(solution)/shard_map/slice | solution.py:16
  147.6 2.7 %slice.33 = f32[1,64,3072]{2,1,0:T(8,128)} reshape(f32[1,64,3,16,1,64]{5,3,2,1,4,0:T(8,128)} %copy.67) | data formatting | bytes 1572864 | tf_op jit(solution)/shard_map/slice | solution.py:16
  150.4 2.2 %collective-permute-start = (f32[1,64,3072]{2,1,0:T(8,128)}, f32[1,64,3072]{2,1,0:T(8,128)}, u32[]{:S(2)}, u32[]{:S(2)}) collective-permute-start(f32[1,64,3072]{2,1,0:T(8,128)} %slice.33), channel_id=1, source_target_pairs={{0,1},{1,2},{2,3},{3,4},{4,5},{5,6},{6,7},{7,8},{8,9},{9,10},{10,1... | collective-permute-start | bytes 2359304 | tf_op jit(solution)/shard_map/ppermute | solution.py:19
  152.5 3.7 %copy.70 = f32[1,64,3,16,1,64]{5,3,2,1,4,0:T(8,128)} copy(f32[1,64,3,16,1,64]{5,2,1,0,3,4:T(4,128)} %get-tuple-element.6) | data formatting | bytes 1572864 | tf_op jit(solution)/shard_map/slice | solution.py:15
  156.2 2.7 %slice.36 = f32[1,64,3072]{2,1,0:T(8,128)} reshape(f32[1,64,3,16,1,64]{5,3,2,1,4,0:T(8,128)} %copy.70) | data formatting | bytes 1572864 | tf_op jit(solution)/shard_map/slice | solution.py:15
  158.9 9.6 %collective-permute-start.1 = (f32[1,64,3072]{2,1,0:T(8,128)}, f32[1,64,3072]{2,1,0:T(8,128)}, u32[]{:S(2)}, u32[]{:S(2)}) collective-permute-start(f32[1,64,3072]{2,1,0:T(8,128)} %slice.36), channel_id=1, source_target_pairs={{1,0},{2,1},{3,2},{4,3},{5,4},{6,5},{7,6},{8,7},{9,8},{10,9},{11,1... | collective-permute-start | bytes 2359304 | tf_op jit(solution)/shard_map/ppermute | solution.py:21
  168.6 2.1 %copy.79 = f32[1,64,3,16,1,64]{5,3,2,1,4,0:T(8,128)} copy(f32[1,64,3,16,1,64]{5,2,1,0,3,4:T(4,128)S(1)} %get-tuple-element.7) | data formatting | bytes 1572864 | tf_op jit(solution)/shard_map/reshape;squeeze | solution.py:85
  170.6 1.9 reshape.200
  172.5 6.0 %collective-permute-done = f32[1,64,3072]{2,1,0:T(8,128)} collective-permute-done((f32[1,64,3072]{2,1,0:T(8,128)}, f32[1,64,3072]{2,1,0:T(8,128)}, u32[]{:S(2)}, u32[]{:S(2)}) %collective-permute-start) | collective-permute-done | bytes 786464 | tf_op jit(solution)/shard_map/ppermute | solution.py:19
  178.5 1.7 reshape_squeeze.9
  180.2 6.6 %collective-permute-done.1 = f32[1,64,3072]{2,1,0:T(8,128)} collective-permute-done((f32[1,64,3072]{2,1,0:T(8,128)}, f32[1,64,3072]{2,1,0:T(8,128)}, u32[]{:S(2)}, u32[]{:S(2)}) %collective-permute-start.1) | collective-permute-done | bytes 786464 | tf_op jit(solution)/shard_map/ppermute | solution.py:21
  186.8 1.7 reshape_squeeze.11
  188.5 0.8 pad_add_fusion
  189.3 1.8 copy.82
  (34 shorter events, 5.3 us)
Async XLA Ops:
  6.5 88.5 %all-gather.3.cloned.1.call-start = ((), (), s32[]{:S(2)}) async-start(), calls=%async_computation | async-start | bytes 2228224 | tf_op jit(solution)/shard_map/all_gather | solution.py:62
  12.1 1.2 copy-start.1
  12.1 40.6 %copy-start = (f32[4,64,256]{2,1,0:T(8,128)S(1)}, f32[4,64,256]{2,1,0:T(8,128)}, u32[]{:S(2)}) copy-start(f32[4,64,256]{2,1,0:T(8,128)} %param.5) | copy-start | bytes 786436
  150.4 28.1 %collective-permute-start = (f32[1,64,3072]{2,1,0:T(8,128)}, f32[1,64,3072]{2,1,0:T(8,128)}, u32[]{:S(2)}, u32[]{:S(2)}) collective-permute-start(f32[1,64,3072]{2,1,0:T(8,128)} %slice.33), channel_id=1, source_target_pairs={{0,1},{1,2},{2,3},{3,4},{4,5},{5,6},{6,7},{7,8},{8,9},{9,10},{10,1... | collective-permute-start | bytes 2359304 | tf_op jit(solution)/shard_map/ppermute | solution.py:19
  158.9 27.9 %collective-permute-start.1 = (f32[1,64,3072]{2,1,0:T(8,128)}, f32[1,64,3072]{2,1,0:T(8,128)}, u32[]{:S(2)}, u32[]{:S(2)}) collective-permute-start(f32[1,64,3072]{2,1,0:T(8,128)} %slice.36), channel_id=1, source_target_pairs={{1,0},{2,1},{3,2},{4,3},{5,4},{6,5},{7,6},{8,7},{9,8},{10,9},{11,1... | collective-permute-start | bytes 2359304 | tf_op jit(solution)/shard_map/ppermute | solution.py:21
Sparse Core Ops, SparseCore 0:
  9.4 85.5 all-gather.2
where the time goes:
time: 199 us; the launch traced here: 198 us
  waiting for transfers between devices  53.3 us (27%)
  local copies, waits for them, and re-layouts  52.1 us (26%)
  blocking collectives  38.1 us (19%)
  matrix products  27.8 us (14%)
  between operations  13.6 us (7%)
  starting transfers between devices  11.8 us (6%)
    all_gather x1, waiting for transfers between devices, body(): portion_blocks = lax.all_gather(prolong_blocks, 'blk', axis=0, tiled=True)  40 us
    all_gather x1, blocking collectives, body(): portion_code = lax.all_gather(prolong_code, 'blk', axis=0, tiled=True)  38.1 us
    slice x3, local copies, waits for them, and re-layouts, with_halo(): lax.slice_in_dim(cells, cells.shape[dim] - width, cells.shape[dim], axis=...  10.7 us
    ppermute x1, starting transfers between devices, with_halo(): lax.ppermute(head, axis, [((i + 1) % count, i) for i in range(count)])  9.65 us
    dot_general x2, matrix products, expand_codes(): jnp.einsum('...anx,...nj->...ajx', shaped, picker, precision=precise)  7.67 us
    reshape x1, local copies, waits for them, and re-layouts, body(): collected.reshape(groups, 3, coarse_height, 3, CB, block_width)  7.44 us
    dot_general x1, matrix products, body(): product = jnp.einsum('qsab,qsby->qsay', picked, gathered, precision=precise)  7.38 us
    dot_general x1, matrix products, body(): collected = jnp.einsum('rj,qry->qjy', restrict, applied, precision=precise)  6.67 us
  transfers between devices with their start and end apart: 3, of which 3 were waited for; matrix products, arithmetic and copies ran while one was open for 11% of the time, Pallas kernels for 0%

commit v1 on v0

v1 whole, which is shorter than its diff:
```python
import jax
import jax.numpy as jnp
from jax import lax
from jax.experimental import pallas as pl
from jax.experimental.pallas import tpu as pltpu
from jax.sharding import PartitionSpec as P

MESH = pl.DeviceIdType.MESH
F32 = jnp.float32
BF16 = jnp.bfloat16

B = 64
FB = 4
KA = 4
NX = 4
NY = 4
PACK = FB * B + 8
HEAD = 136
STEPS = NX * NY // 2


def kernel(
    a_ref, p_ref, group_ref, row_ref, code_ref, out_ref,
    held, left_hi, left_lo, win_hi, win_lo, middle, up_out, down_out, lower, upper,
    pair_tab, row_tab,
    y_send, y_recv, x_send, x_recv, h_send, h_recv, halo_send, halo_recv,
):
    blk, band = lax.axis_index("blk"), lax.axis_index("band")
    bands = lax.axis_size("band")
    y, x = blk // NX, blk % NX
    right, left = (x + 1) % NX, (x + NX - 1) % NX
    above, below = (band + 1) % bands, (band + bands - 1) % bands
    lane = lax.broadcasted_iota(jnp.int32, (B, 2 * B), 1)
    first_half = lane < B

    def at(row, column):
        return (row * NX + column, band)

    barrier = pltpu.get_barrier_semaphore()
    for target in (at(y, right), at(y, left), (blk, above), (blk, below)):
        pl.semaphore_signal(barrier, inc=1, device_id=target, device_id_type=MESH)

    @pl.when(y < NY - 1)
    def _():
        pl.semaphore_signal(barrier, inc=1, device_id=at(y + 1, x), device_id_type=MESH)

    @pl.when(y > 0)
    def _():
        pl.semaphore_signal(barrier, inc=1, device_id=at(y - 1, x), device_id_type=MESH)

    held[blk, 0 : FB * B, :] = p_ref[...].reshape(FB * B, 2 * B)
    tile_row = lax.broadcasted_iota(jnp.int32, (8, 2 * B), 0)
    tile_lane = lax.broadcasted_iota(jnp.int32, (8, 2 * B), 1)
    codes = jnp.zeros((8, 2 * B), F32)
    for i in range(FB):
        one = jnp.where(tile_lane < B, code_ref[i, 0], code_ref[i, 1]).astype(F32)
        codes = jnp.where(tile_row == i, one, codes)
    held[blk, FB * B : PACK, :] = codes

    pl.semaphore_wait(barrier, 4 + jnp.where(y < NY - 1, 1, 0) + jnp.where(y > 0, 1, 0))

    def y_copy(source, target, sender):
        slot = held.at[source * NX + x]
        return pltpu.make_async_remote_copy(
            src_ref=slot, dst_ref=slot, send_sem=y_send.at[sender], recv_sem=y_recv.at[source],
            device_id=at(target, x), device_id_type=MESH,
        )

    def x_copy(source, column, side):
        slot = held.at[source * NX + column]
        return pltpu.make_async_remote_copy(
            src_ref=slot, dst_ref=slot, send_sem=x_send.at[side, source], recv_sem=x_recv.at[side, source],
            device_id=at(y, left if side else right), device_id_type=MESH,
        )

    def h_copy(source, column, side):
        rows = pl.ds(HEAD, PACK - HEAD) if side else pl.ds(0, HEAD)
        slot = held.at[source * NX + column, rows]
        return pltpu.make_async_remote_copy(
            src_ref=slot, dst_ref=slot, send_sem=h_send.at[side, source], recv_sem=h_recv.at[side, source],
            device_id=at(y, left if side else right), device_id_type=MESH,
        )

    def halo_copy(step, side):
        return pltpu.make_async_remote_copy(
            src_ref=(down_out if side else up_out).at[step], dst_ref=(upper if side else lower).at[step],
            send_sem=halo_send.at[side, step], recv_sem=halo_recv.at[side, step],
            device_id=(blk, below if side else above), device_id_type=MESH,
        )

    order = [
        y,
        jnp.where(y == 0, 1, y - 1),
        jnp.where(y == 0, 2, jnp.where(y == 3, 1, y + 1)),
        jnp.where(y < 2, 3, 0),
    ]

    def onward(source):
        return jnp.where(source < y, y + 1, y - 1)

    def inside(target):
        return (target >= 0) & (target < NY)

    def x_start(source):
        x_copy(source, x, 0).start()
        x_copy(source, x, 1).start()

    def y_take(turn):
        source = order[turn]
        y_copy(source, jnp.where(source < y, y - 1, y + 1), 1 + turn).wait_recv()
        target = onward(source)

        @pl.when(inside(target))
        def _():
            y_copy(source, target, 1 + turn).start()

        x_start(source)

    def x_take(turn):
        source = order[turn]
        x_copy(source, left, 0).wait_recv()
        h_copy(source, left, 0).start()
        x_copy(source, right, 1).wait_recv()
        h_copy(source, right, 1).start()

    def h_take(turn):
        source = order[turn]
        far = (x + 2) % NX
        h_copy(source, far, 0).wait_recv()
        h_copy(source, far, 1).wait_recv()

    @pl.when(y < NY - 1)
    def _():
        y_copy(y, y + 1, 0).start()

    @pl.when(y > 0)
    def _():
        y_copy(y, y - 1, 1).start()

    x_start(y)

    def tabulate(group, carry):
        pair = [jnp.int32(0), jnp.int32(0)]
        row = [jnp.int32(FB), jnp.int32(FB)]
        for at_pair in range(FB * KA - 1, -1, -1):
            i, k = at_pair // KA, at_pair % KA
            hit = group_ref[i, k] == group
            pair = [jnp.where(hit, at_pair, pair[0]), jnp.where(hit, pair[0], pair[1])]
            row = [jnp.where(hit, row_ref[i, k], row[0]), jnp.where(hit, row[0], row[1])]
        for slot in range(2):
            pair_tab[2 * group + slot] = pair[slot]
            row_tab[2 * group + slot] = row[slot]
        return carry

    lax.fori_loop(0, NX * NY, tabulate, 0)

    def windowed(values, code, at_code):
        chosen = jnp.where(code == at_code, values, 0.0)
        return chosen + pltpu.roll(chosen, B, 1)

    def left_product(i, carry):
        p_here = p_ref[i]
        code = jnp.broadcast_to(held[blk, pl.ds(FB * B + i, 1), :], (B, 2 * B)).astype(jnp.int32)
        parts = [windowed(p_here, code, d) for d in range(3)]
        restrict = jnp.concatenate(
            [jnp.where(first_half, parts[0], parts[1]), jnp.where(first_half, parts[2], 0.0)], axis=1
        )
        twice = []
        for side in range(2):
            both = a_ref[i, :, side * 2 * B : (side + 1) * 2 * B]
            turned = pltpu.roll(both, B, 1)
            twice += [jnp.where(first_half, both, turned), jnp.where(first_half, turned, both)]
        result = lax.dot_general(
            restrict, jnp.concatenate(twice, axis=1), (((0,), (0,)), ((), ())),
            precision=lax.Precision.HIGHEST, preferred_element_type=F32,
        )[0 : 3 * B]
        high = result.astype(BF16)
        low = (result - high.astype(F32)).astype(BF16)
        for k in range(KA):
            left_hi[i * KA + k] = high[:, k * 2 * B : (k + 1) * 2 * B]
            left_lo[i * KA + k] = low[:, k * 2 * B : (k + 1) * 2 * B]
        return carry

    lax.fori_loop(0, FB, left_product, 0)

    wide_half = lax.broadcasted_iota(jnp.int32, (3 * B, 2 * B), 1) < B

    def compute(step):
        for half in range(2):
            group = 2 * step + half
            here = [held[group, i * B : (i + 1) * B, :] for i in range(FB)]
            tile = held[group, FB * B : PACK, :]
            for slot in range(2):
                row = row_tab[2 * group + slot]
                picks = [jnp.where(row == i, 1.0, 0.0).astype(F32) for i in range(FB)]
                values = sum(picks[i] * here[i] for i in range(FB))
                code = sum(picks[i] * tile[i : i + 1, :] for i in range(FB))
                code = jnp.broadcast_to(code, (B, 2 * B)).astype(jnp.int32)
                mine = first_half if half == 0 else jnp.logical_not(first_half)
                at_row = (2 * half + slot) * B
                for e in range(3):
                    part = jnp.where(mine, windowed(values, code, e), 0.0)
                    high = part.astype(BF16)
                    win_hi[at_row : at_row + B, e * 2 * B : (e + 1) * 2 * B] = high
                    win_lo[at_row : at_row + B, e * 2 * B : (e + 1) * 2 * B] = (part - high.astype(F32)).astype(BF16)

        def stacked(ref):
            pairs = [ref[pair_tab[4 * step + n]] for n in range(4)]
            return jnp.concatenate(
                [jnp.where(wide_half, pairs[0], pairs[1]), jnp.where(wide_half, pairs[2], pairs[3])], axis=1
            )

        high, low = stacked(left_hi), stacked(left_lo)
        total = jnp.dot(high, win_hi[...], preferred_element_type=F32)
        total += jnp.dot(high, win_lo[...], preferred_element_type=F32)
        total += jnp.dot(low, win_hi[...], preferred_element_type=F32)
        down_out[step] = total[0:B]
        middle[step] = total[B : 2 * B]
        up_out[step] = total[2 * B : 3 * B]
        halo_copy(step, 0).start()
        halo_copy(step, 1).start()

    def finish(step):
        halo_copy(step, 0).wait_recv()
        halo_copy(step, 1).wait_recv()
        for e in range(5):
            parts = []
            for ref, shift in ((lower, 0), (middle, 1), (upper, 2)):
                if 0 <= e - shift < 3:
                    parts.append(ref[step, :, (e - shift) * 2 * B : (e - shift + 1) * 2 * B])
            column = pl.multiple_of(e * NX * NY * B + step * 2 * B, 2 * B)
            out_ref[:, pl.ds(column, 2 * B)] = sum(parts[1:], parts[0])

    def both_steps(work, turn):
        def one(n, carry):
            work(2 * order[turn] + n)
            return carry

        lax.fori_loop(0, 2, one, 0)

    y_take(1)
    x_take(0)
    y_take(2)
    h_take(0)
    both_steps(compute, 0)
    x_take(1)
    y_take(3)
    x_take(2)
    h_take(1)
    both_steps(compute, 1)
    x_take(3)
    h_take(2)
    both_steps(compute, 2)
    both_steps(finish, 0)
    h_take(3)
    both_steps(compute, 3)
    for turn in range(1, 4):
        both_steps(finish, turn)

    @pl.when(y < NY - 1)
    def _():
        y_copy(y, y + 1, 0).wait_send()

    @pl.when(y > 0)
    def _():
        y_copy(y, y - 1, 1).wait_send()

    for turn in range(1, 4):
        target = onward(order[turn])

        @pl.when(inside(target))
        def _():
            y_copy(order[turn], target, 1 + turn).wait_send()

    def drain_x(source, carry):
        for side, column in ((0, left), (1, right)):
            x_copy(source, x, side).wait_send()
            h_copy(source, column, side).wait_send()
        return carry

    lax.fori_loop(0, NY, drain_x, 0)

    def drain_halo(step, carry):
        halo_copy(step, 0).wait_send()
        halo_copy(step, 1).wait_send()
        return carry

    lax.fori_loop(0, STEPS, drain_halo, 0)


def body(fine_blocks, source_group, source_row, prolong_blocks, prolong_code):
    vmem = pl.BlockSpec(memory_space=pltpu.VMEM)
    smem = pl.BlockSpec(memory_space=pltpu.SMEM)
    window = 3 * 2 * B
    halo = pltpu.VMEM((STEPS, B, window), F32)
    dma = pltpu.SemaphoreType.DMA
    return pl.pallas_call(
        kernel,
        out_shape=jax.ShapeDtypeStruct((B, 5 * NX * NY * B), F32),
        in_specs=[vmem, vmem, smem, smem, smem],
        out_specs=vmem,
        scratch_shapes=[
            pltpu.VMEM((NX * NY, PACK, 2 * B), F32),
            pltpu.VMEM((FB * KA, 3 * B, 2 * B), BF16),
            pltpu.VMEM((FB * KA, 3 * B, 2 * B), BF16),
            pltpu.VMEM((4 * B, window), BF16),
            pltpu.VMEM((4 * B, window), BF16),
            halo, halo, halo, halo, halo,
            pltpu.SMEM((2 * NX * NY,), jnp.int32),
            pltpu.SMEM((2 * NX * NY,), jnp.int32),
            dma((5,)), dma((NY,)),
            dma((2, NY)), dma((2, NY)),
            dma((2, NY)), dma((2, NY)),
            dma((2, STEPS)), dma((2, STEPS)),
        ],
        compiler_params=pltpu.CompilerParams(
            collective_id=0, has_side_effects=True, vmem_limit_bytes=40 * 2**20
        ),
        cost_estimate=pl.CostEstimate(flops=10**9, bytes_accessed=4 * 2**20, transcendentals=0),
        name="galerkin",
    )(fine_blocks, prolong_blocks, source_group, source_row, prolong_code)


def solution(mesh):
    return jax.shard_map(
        body,
        mesh=mesh,
        in_specs=(
            P(("blk", "band"), None, None),
            P(("blk", "band"), None),
            P(("blk", "band"), None),
            P(("blk", "band"), None, None),
            P(("blk", "band"), None),
        ),
        out_specs=P(("blk", "band"), None),
        check_vma=False,
    )
```

time: 199 us -> 53.6 us (0.27)
  waiting for transfers between devices: 53.3 us -> 0 us
  Pallas kernels: 0 us -> 48.3 us
  local copies, waits for them, and re-layouts: 52.1 us -> 5.04 us
  blocking collectives: 38.1 us -> 0 us
  matrix products: 27.8 us -> 0 us
  between operations: 13.6 us -> 0.01 us
  starting transfers between devices: 11.8 us -> 0 us
    pallas_call x0 -> x1, Pallas kernels: none -> 48.3 us  [body(): pl.pallas_call(kernel, out_shape=jax.ShapeDtypeStruct((B, 5 * NX * NY * B...]
    all_gather x1 -> x0, waiting for transfers between devices: 40 us -> none  [body(): portion_blocks = lax.all_gather(prolong_blocks, 'blk', axis=0, tiled=True)]
    all_gather x1 -> x0, blocking collectives: 38.1 us -> none  [body(): portion_code = lax.all_gather(prolong_code, 'blk', axis=0, tiled=True)]
    dot_general x5 -> x0, matrix products: 27.8 us -> none  [the longest x2 7.67 us: expand_codes(): jnp.einsum('...anx,...nj->...ajx', shaped, picker, precision=precise)]
    slice x6 -> x0, local copies, waits for them, and re-layouts: 17.2 us -> none  [the longest x3 10.7 us: with_halo(): lax.slice_in_dim(cells, cells.shape[dim] - width, cells.shape[dim], axis=...]
    ppermute x2 -> x0, waiting for transfers between devices: 12.6 us -> none  [the longest x1 6.61 us: with_halo(): lax.ppermute(head, axis, [((i + 1) % count, i) for i in range(count)])]
    ppermute x2 -> x0, starting transfers between devices: 11.8 us -> none  [the longest x1 9.65 us: with_halo(): lax.ppermute(head, axis, [((i + 1) % count, i) for i in range(count)])]
    reshape x4 -> x0, local copies, waits for them, and re-layouts: 10.5 us -> none  [the longest x1 7.44 us: body(): collected.reshape(groups, 3, coarse_height, 3, CB, block_width)]
  transfers between devices with their start and end apart: 3 -> 0, of which waited for: 3 -> 0; matrix products, arithmetic and copies ran while one was open for 11% -> 0% of each run, Pallas kernels for 0% -> 0%
where the time goes in v1:
time: 53.6 us; the launch traced here: 53.4 us
  Pallas kernels  48.3 us (90%)
  local copies, waits for them, and re-layouts  5.04 us (9%)
    pallas_call x1, Pallas kernels, body(): pl.pallas_call(kernel, out_shape=jax.ShapeDtypeStruct((B, 5 * NX * NY * B...  48.3 us
    unnamed x10, local copies, waits for them, and re-layouts  5.04 us

profile of v1, /device:TPU:6, one launch (start us, length us, event | category | flops | bytes accessed | tf_op | source)
XLA Modules:
  0.0 53.4 jit_solution(5741923937824415072)
XLA Ops:
  0.0 0.8 %copy.6.code_ref = s32[4,2]{1,0:T(4,128)S(1)} copy(s32[4,2]{0,1:T(2,128)} %param.9) | data formatting | bytes 64 | tf_op args[4]
  0.8 0.0 copy-start
  0.8 0.9 %copy-done = f32[4,64,256]{2,1,0:T(8,128)S(1)} copy-done((f32[4,64,256]{2,1,0:T(8,128)S(1)}, f32[4,64,256]{2,1,0:T(8,128)}, u32[]{:S(2)}) %copy-start) | copy-done | bytes 262168
  1.7 0.0 copy-start.1
  1.7 0.9 %copy-done.1 = f32[4,64,128]{2,1,0:T(8,128)S(1)} copy-done((f32[4,64,128]{2,1,0:T(8,128)S(1)}, f32[4,64,128]{2,1,0:T(8,128)}, u32[]{:S(2)}) %copy-start.1) | copy-done | bytes 131096
  2.6 0.0 copy-start.2
  2.6 0.7 %copy-done.2 = s32[4,4]{1,0:T(4,128)S(1)} copy-done((s32[4,4]{1,0:T(4,128)S(1)}, s32[4,4]{1,0:T(4,128)}, u32[]{:S(2)}) %copy-start.2) | copy-done | bytes 88
  3.3 0.0 copy-start.3
  3.3 0.7 %copy-done.3 = s32[4,4]{1,0:T(4,128)S(1)} copy-done((s32[4,4]{1,0:T(4,128)S(1)}, s32[4,4]{1,0:T(4,128)}, u32[]{:S(2)}) %copy-start.3) | copy-done | bytes 88
  4.0 48.3 %galerkin.1 = f32[64,5120]{1,0:T(8,128)S(1)} custom-call(f32[4,64,256]{2,1,0:T(8,128)S(1)} %copy-done, f32[4,64,128]{2,1,0:T(8,128)S(1)} %copy-done.1, s32[4,4]{1,0:T(4,128)S(1)} %copy-done.2, s32[4,4]{1,0:T(4,128)S(1)} %copy-done.3, s32[4,2]{1,0:T(4,128)S(1)} %copy.6.code_ref), custom_call_target="tpu_custom_call" | custom-call | flops 1000000000 | bytes 4194304 | tf_op jit(solution)/shard_map/galerkin/pallas_call | solution.py:297
  52.3 1.1 %copy.8 = f32[64,5120]{1,0:T(8,128)} copy(f32[64,5120]{1,0:T(8,128)S(1)} %galerkin.1) | data formatting | bytes 2621440
Async XLA Ops:
  0.8 0.9 %copy-start = (f32[4,64,256]{2,1,0:T(8,128)S(1)}, f32[4,64,256]{2,1,0:T(8,128)}, u32[]{:S(2)}) copy-start(f32[4,64,256]{2,1,0:T(8,128)} %a_ref.1) | copy-start | bytes 786436
  1.7 0.9 %copy-start.1 = (f32[4,64,128]{2,1,0:T(8,128)S(1)}, f32[4,64,128]{2,1,0:T(8,128)}, u32[]{:S(2)}) copy-start(f32[4,64,128]{2,1,0:T(8,128)} %p_ref.1) | copy-start | bytes 393220
  2.6 0.7 %copy-start.2 = (s32[4,4]{1,0:T(4,128)S(1)}, s32[4,4]{1,0:T(4,128)}, u32[]{:S(2)}) copy-start(s32[4,4]{1,0:T(4,128)} %group_ref.1) | copy-start | bytes 196
  3.3 0.7 %copy-start.3 = (s32[4,4]{1,0:T(4,128)S(1)}, s32[4,4]{1,0:T(4,128)}, u32[]{:S(2)}) copy-start(s32[4,4]{1,0:T(4,128)} %row_ref.1) | copy-start | bytes 196

commit v2 on v1

v2 whole, which is shorter than its diff:
```python
import jax
import jax.numpy as jnp
from jax import lax
from jax.experimental import pallas as pl
from jax.experimental.pallas import tpu as pltpu
from jax.sharding import PartitionSpec as P

MESH = pl.DeviceIdType.MESH
F32 = jnp.float32
BF16 = jnp.bfloat16

B = 64
FB = 4
KA = 4
MB = 2
NX = 4
NY = 4
PACK = FB * B + 8
SHARE = MB * B + 8
STEPS = NX * NY // 2


def kernel(
    a_hbm, p_hbm, group_hbm, row_hbm, code_hbm, out_ref,
    a_ref, group_ref, row_ref, code_ref,
    held, want, asked, staged, got, left_hi, left_lo, win_hi, win_lo,
    middle, up_out, down_out, lower, upper, pair_tab,
    in_sem, y_send, y_recv, ask_send, ask_recv, x_send, x_recv, halo_send, halo_recv, ready,
):
    blk, band = lax.axis_index("blk"), lax.axis_index("band")
    bands = lax.axis_size("band")
    half_bands = bands // 2
    y, x = blk // NX, blk % NX
    above, below = (band + 1) % bands, (band + bands - 1) % bands
    is_first, is_last = band % half_bands == 0, band % half_bands == half_bands - 1
    lane = lax.broadcasted_iota(jnp.int32, (B, 2 * B), 1)
    first_half = lane < B

    def at(row, column):
        return (row * NX + column, band)

    def beside(shift):
        return (x + shift) % NX

    def signal(semaphore, target):
        pl.semaphore_signal(semaphore, inc=1, device_id=target, device_id_type=MESH)

    inputs = [
        pltpu.make_async_copy(source, target, in_sem.at[n])
        for n, (source, target) in enumerate((
            (group_hbm, group_ref), (row_hbm, row_ref), (code_hbm, code_ref),
            (p_hbm, held.at[y, pl.ds(0, FB * B)]), (a_hbm, a_ref),
        ))
    ]
    for copy in inputs:
        copy.start()

    barrier = pltpu.get_barrier_semaphore()
    for shift in range(1, NX):
        signal(barrier, at(y, beside(shift)))

    @pl.when(y < NY - 1)
    def _():
        signal(barrier, at(y + 1, x))

    @pl.when(y > 0)
    def _():
        signal(barrier, at(y - 1, x))

    @pl.when(jnp.logical_not(is_last))
    def _():
        signal(barrier, (blk, above))

    @pl.when(is_first)
    def _():
        signal(barrier, (blk, below))

    for copy in inputs[0:2]:
        copy.wait()

    def tabulate(group, carry):
        pair = [jnp.int32(0), jnp.int32(0)]
        row = [jnp.int32(FB), jnp.int32(FB)]
        for at_pair in range(FB * KA - 1, -1, -1):
            i, k = at_pair // KA, at_pair % KA
            hit = group_ref[i, k] == group
            pair = [jnp.where(hit, at_pair, pair[0]), jnp.where(hit, pair[0], pair[1])]
            row = [jnp.where(hit, row_ref[i, k], row[0]), jnp.where(hit, row[0], row[1])]
        for slot in range(MB):
            pair_tab[MB * group + slot] = pair[slot]
            want[group % NX, pl.ds(MB * (group // NX) + slot, 1), :] = jnp.full((1, 2 * B), row[slot]).astype(F32)
        return carry

    lax.fori_loop(0, NX * NY, tabulate, 0)

    inputs[2].wait()
    tile_row = lax.broadcasted_iota(jnp.int32, (8, 2 * B), 0)
    tile_lane = lax.broadcasted_iota(jnp.int32, (8, 2 * B), 1)
    codes = jnp.zeros((8, 2 * B), F32)
    for i in range(FB):
        one = jnp.where(tile_lane < B, code_ref[0, i], code_ref[1, i]).astype(F32)
        codes = jnp.where(tile_row == i, one, codes)
    held[y, FB * B : PACK, :] = codes
    inputs[3].wait()

    pl.semaphore_wait(
        barrier,
        NX - 1 + jnp.where(y < NY - 1, 1, 0) + jnp.where(y > 0, 1, 0)
        + jnp.where(is_first, 0, 1) + jnp.where(is_last, 1, 0),
    )

    def y_copy(source, target, sender):
        slot = held.at[source]
        return pltpu.make_async_remote_copy(
            src_ref=slot, dst_ref=slot, send_sem=y_send.at[sender], recv_sem=y_recv.at[source],
            device_id=at(target, x), device_id_type=MESH,
        )

    def ask_copy(shift):
        return pltpu.make_async_remote_copy(
            src_ref=want.at[beside(shift)], dst_ref=asked.at[NX - shift],
            send_sem=ask_send.at[shift], recv_sem=ask_recv.at[NX - shift],
            device_id=at(y, beside(shift)), device_id_type=MESH,
        )

    def x_copy(source, shift):
        return pltpu.make_async_remote_copy(
            src_ref=staged.at[shift, source], dst_ref=got.at[x, source],
            send_sem=x_send.at[shift, source], recv_sem=x_recv.at[shift, source],
            device_id=at(y, beside(shift)), device_id_type=MESH,
        )

    def x_landing(source, shift):
        return pltpu.make_async_remote_copy(
            src_ref=staged.at[shift, source], dst_ref=got.at[beside(NX - shift), source],
            send_sem=x_send.at[shift, source], recv_sem=x_recv.at[shift, source],
            device_id=at(y, beside(shift)), device_id_type=MESH,
        )

    def ask_landing(shift):
        return pltpu.make_async_remote_copy(
            src_ref=want.at[beside(shift)], dst_ref=asked.at[shift],
            send_sem=ask_send.at[shift], recv_sem=ask_recv.at[shift],
            device_id=at(y, beside(shift)), device_id_type=MESH,
        )

    def halo_copy(step, side):
        return pltpu.make_async_remote_copy(
            src_ref=(down_out if side else up_out).at[step], dst_ref=(upper if side else lower).at[step],
            send_sem=halo_send.at[side, step], recv_sem=halo_recv.at[side, step],
            device_id=(blk, below if side else above), device_id_type=MESH,
        )

    order = [
        y,
        jnp.where(y == 0, 1, y - 1),
        jnp.where(y == 0, 2, jnp.where(y == 3, 1, y + 1)),
        jnp.where(y < 2, 3, 0),
    ]

    def onward(source):
        return jnp.where(source < y, y + 1, y - 1)

    def inside(target):
        return (target >= 0) & (target < NY)

    def serve(turn):
        source = order[turn]

        def choose(wanted, slot, target):
            row = wanted(MB * source + slot)
            pick = jnp.broadcast_to(row, (B, 2 * B))
            values = jnp.zeros((B, 2 * B), F32)
            code = jnp.zeros((1, 2 * B), F32)
            for i in range(FB):
                values = jnp.where(pick == i, held[source, i * B : (i + 1) * B, :], values)
                code = jnp.where(row == i, held[source, FB * B + i : FB * B + i + 1, :], code)
            target(slice(slot * B, (slot + 1) * B), values)
            target(slice(MB * B + slot, MB * B + slot + 1), code)

        for shift in (2, 1, 3):
            for slot in range(MB):

                def wanted(n, shift=shift):
                    return asked[shift, pl.ds(n, 1), :]

                def target(rows, values, shift=shift):
                    staged[shift, source, rows, :] = values

                choose(wanted, slot, target)
            x_copy(source, shift).start()
        for slot in range(MB):

            def own(n):
                return want[x, pl.ds(n, 1), :]

            def keep(rows, values):
                got[x, source, rows, :] = values

            choose(own, slot, keep)

    def y_take(turn):
        source = order[turn]
        y_copy(source, jnp.where(source < y, y - 1, y + 1), 1 + turn).wait_recv()
        target = onward(source)

        @pl.when(inside(target))
        def _():
            y_copy(source, target, 1 + turn).start()

        serve(turn)

    def x_take(turn):
        for shift in range(1, NX):
            x_landing(order[turn], shift).wait_recv()

    @pl.when(y < NY - 1)
    def _():
        y_copy(y, y + 1, 0).start()

    @pl.when(y > 0)
    def _():
        y_copy(y, y - 1, 1).start()

    for shift in (2, 1, 3):
        ask_copy(shift).start()

    @pl.when(jnp.logical_not(is_first))
    def _():
        signal(ready.at[0], (blk, below))

    @pl.when(is_last)
    def _():
        signal(ready.at[1], (blk, above))

    def windowed(values, code, at_code):
        chosen = jnp.where(code == at_code, values, 0.0)
        return chosen + pltpu.roll(chosen, B, 1)

    def left_product(i, carry):
        p_here = held[y, pl.ds(pl.multiple_of(i * B, B), B), :]
        code = jnp.broadcast_to(held[y, pl.ds(FB * B + i, 1), :], (B, 2 * B))
        parts = [windowed(p_here, code, d) for d in range(3)]
        restrict = jnp.concatenate(
            [jnp.where(first_half, parts[0], parts[1]), jnp.where(first_half, parts[2], 0.0)], axis=1
        )
        twice = []
        for side in range(2):
            both = a_ref[i, :, side * 2 * B : (side + 1) * 2 * B]
            turned = pltpu.roll(both, B, 1)
            twice += [jnp.where(first_half, both, turned), jnp.where(first_half, turned, both)]
        result = lax.dot_general(
            restrict, jnp.concatenate(twice, axis=1), (((0,), (0,)), ((), ())),
            precision=lax.Precision.HIGHEST, preferred_element_type=F32,
        )[0 : 3 * B]
        high = result.astype(BF16)
        low = (result - high.astype(F32)).astype(BF16)
        for k in range(KA):
            left_hi[i * KA + k] = high[:, k * 2 * B : (k + 1) * 2 * B]
            left_lo[i * KA + k] = low[:, k * 2 * B : (k + 1) * 2 * B]
        return carry

    wide_half = lax.broadcasted_iota(jnp.int32, (3 * B, 2 * B), 1) < B

    def compute(step):
        for half in range(2):
            row, column = step // 2, 2 * (step % 2) + half
            for slot in range(MB):
                values = got[column, row, slot * B : (slot + 1) * B, :]
                code = jnp.broadcast_to(got[column, row, MB * B + slot : MB * B + slot + 1, :], (B, 2 * B))
                mine = first_half if half == 0 else jnp.logical_not(first_half)
                at_row = (MB * half + slot) * B
                for e in range(3):
                    part = jnp.where(mine, windowed(values, code, e), 0.0)
                    high = part.astype(BF16)
                    win_hi[at_row : at_row + B, e * 2 * B : (e + 1) * 2 * B] = high
                    win_lo[at_row : at_row + B, e * 2 * B : (e + 1) * 2 * B] = (part - high.astype(F32)).astype(BF16)

        def stacked(ref):
            pairs = [ref[pair_tab[2 * MB * step + n]] for n in range(2 * MB)]
            return jnp.concatenate(
                [jnp.where(wide_half, pairs[0], pairs[1]), jnp.where(wide_half, pairs[2], pairs[3])], axis=1
            )

        high, low = stacked(left_hi), stacked(left_lo)
        total = jnp.dot(high, win_hi[...], preferred_element_type=F32)
        total += jnp.dot(high, win_lo[...], preferred_element_type=F32)
        total += jnp.dot(low, win_hi[...], preferred_element_type=F32)
        down_out[step] = total[0:B]
        middle[step] = total[B : 2 * B]
        up_out[step] = total[2 * B : 3 * B]

    def send_up(step):
        halo_copy(step, 0).start()

    def send_down(step):
        halo_copy(step, 1).start()

    def finish(step):
        halo_copy(step, 0).wait_recv()
        halo_copy(step, 1).wait_recv()
        for e in range(5):
            parts = []
            for ref, shift in ((lower, 0), (middle, 1), (upper, 2)):
                if 0 <= e - shift < 3:
                    parts.append(ref[step, :, (e - shift) * 2 * B : (e - shift + 1) * 2 * B])
            column = pl.multiple_of(e * NX * NY * B + step * 2 * B, 2 * B)
            out_ref[:, pl.ds(column, 2 * B)] = sum(parts[1:], parts[0])

    def both_steps(turn, *work):
        def one(n, carry):
            for each in work:
                each(2 * order[turn] + n)
            return carry

        lax.fori_loop(0, 2, one, 0)

    inputs[4].wait()
    lax.fori_loop(0, 2, left_product, 0)
    for shift in range(1, NX):
        ask_landing(shift).wait_recv()
    serve(0)
    lax.fori_loop(2, 3, left_product, 0)
    y_take(1)
    lax.fori_loop(3, 4, left_product, 0)
    y_take(2)
    x_take(0)

    @pl.when(jnp.logical_not(is_last))
    def _():
        pl.semaphore_wait(ready.at[0], 1)

    both_steps(0, compute, send_up)

    @pl.when(jnp.logical_not(is_first))
    def _():
        both_steps(0, send_down)

    y_take(3)
    x_take(1)
    both_steps(1, compute, send_up)

    @pl.when(is_first)
    def _():
        pl.semaphore_wait(ready.at[1], 1)
        both_steps(0, send_down)

    both_steps(1, send_down)
    x_take(2)
    both_steps(2, compute, send_up, send_down)
    x_take(3)
    both_steps(3, compute, send_up, send_down)
    for turn in range(4):
        both_steps(turn, finish)

    @pl.when(y < NY - 1)
    def _():
        y_copy(y, y + 1, 0).wait_send()

    @pl.when(y > 0)
    def _():
        y_copy(y, y - 1, 1).wait_send()

    for turn in range(1, 4):
        target = onward(order[turn])

        @pl.when(inside(target))
        def _():
            y_copy(order[turn], target, 1 + turn).wait_send()

    for shift in range(1, NX):
        ask_copy(shift).wait_send()

    def drain_x(source, carry):
        for shift in range(1, NX):
            x_copy(source, shift).wait_send()
        return carry

    lax.fori_loop(0, NY, drain_x, 0)

    def drain_halo(step, carry):
        halo_copy(step, 0).wait_send()
        halo_copy(step, 1).wait_send()
        return carry

    lax.fori_loop(0, STEPS, drain_halo, 0)


def body(fine_blocks, source_group, source_row, prolong_blocks, prolong_code):
    hbm = pl.BlockSpec(memory_space=pltpu.HBM)
    window = 3 * 2 * B
    halo = pltpu.VMEM((STEPS, B, window), F32)
    dma = pltpu.SemaphoreType.DMA
    return pl.pallas_call(
        kernel,
        out_shape=jax.ShapeDtypeStruct((B, 5 * NX * NY * B), F32),
        in_specs=[hbm] * 5,
        out_specs=pl.BlockSpec(memory_space=pltpu.VMEM),
        scratch_shapes=[
            pltpu.VMEM((FB, B, KA * B), F32),
            pltpu.SMEM((FB, KA), jnp.int32),
            pltpu.SMEM((FB, KA), jnp.int32),
            pltpu.SMEM((2, FB), jnp.int32),
            pltpu.VMEM((NY, PACK, 2 * B), F32),
            pltpu.VMEM((NX, NY * MB, 2 * B), F32),
            pltpu.VMEM((NX, NY * MB, 2 * B), F32),
            pltpu.VMEM((NX, NY, SHARE, 2 * B), F32),
            pltpu.VMEM((NX, NY, SHARE, 2 * B), F32),
            pltpu.VMEM((FB * KA, 3 * B, 2 * B), BF16),
            pltpu.VMEM((FB * KA, 3 * B, 2 * B), BF16),
            pltpu.VMEM((2 * MB * B, window), BF16),
            pltpu.VMEM((2 * MB * B, window), BF16),
            halo, halo, halo, halo, halo,
            pltpu.SMEM((MB * NX * NY,), jnp.int32),
            dma((5,)),
            dma((5,)), dma((NY,)),
            dma((NX,)), dma((NX,)),
            dma((NX, NY)), dma((NX, NY)),
            dma((2, STEPS)), dma((2, STEPS)),
            pltpu.SemaphoreType.REGULAR((2,)),
        ],
        compiler_params=pltpu.CompilerParams(
            collective_id=0, has_side_effects=True, vmem_limit_bytes=60 * 2**20
        ),
        cost_estimate=pl.CostEstimate(flops=10**9, bytes_accessed=4 * 2**20, transcendentals=0),
        name="galerkin",
    )(fine_blocks, prolong_blocks.reshape(FB * B, 2 * B), source_group, source_row, prolong_code.T)


def solution(mesh):
    return jax.shard_map(
        body,
        mesh=mesh,
        in_specs=(
            P(("blk", "band"), None, None),
            P(("blk", "band"), None),
            P(("blk", "band"), None),
            P(("blk", "band"), None, None),
            P(("blk", "band"), None),
        ),
        out_specs=P(("blk", "band"), None),
        check_vma=False,
    )
```

time: 53.6 us -> 49.9 us (0.931)
  the two profiles are of different devices: /device:TPU:6 before, /device:TPU:8 now
where the time goes in v2:
time: 49.9 us; the launch traced here: 49.8 us
  Pallas kernels  47.3 us (95%)
  local copies, waits for them, and re-layouts  2.47 us (5%)
    pallas_call x1, Pallas kernels, body(): pl.pallas_call(kernel, out_shape=jax.ShapeDtypeStruct((B, 5 * NX * NY * B...  47.3 us
    unnamed x1, local copies, waits for them, and re-layouts  2.47 us

profile of v2, /device:TPU:8, one launch (start us, length us, event | category | flops | bytes accessed | tf_op | source)
XLA Modules:
  0.0 49.8 jit_solution(14152088874431833264)
XLA Ops:
  0.0 47.3 %galerkin.1 = f32[64,5120]{1,0:T(8,128)} custom-call(f32[4,64,256]{2,1,0:T(8,128)} %a_hbm.1, f32[256,128]{1,0:T(8,128)} %bitcast.2, s32[4,4]{1,0:T(4,128)} %group_hbm.1, s32[4,4]{1,0:T(4,128)} %row_hbm.1, s32[2,4]{1,0:T(2,128)} %bitcast.3), custom_call_target="tpu_custom_call" | custom-call | flops 1000000000 | bytes 4194304 | tf_op jit(solution)/shard_map/galerkin/pallas_call | solution.py:394
  47.3 2.5 %copy.7 = f32[64,5120]{1,0:T(8,128)} copy(f32[64,5120]{1,0:T(8,128)} %galerkin.1) | data formatting | bytes 2621440

commit v3 on v2

--- a/solution.py
+++ b/solution.py
@@ -18,21 +18,26 @@
 PACK = FB * B + 8
 SHARE = MB * B + 8
 STEPS = NX * NY // 2
+DETOURS = 4
 
 
 def kernel(
     a_hbm, p_hbm, group_hbm, row_hbm, code_hbm, out_ref,
     a_ref, group_ref, row_ref, code_ref,
     held, want, asked, staged, got, left_hi, left_lo, win_hi, win_lo,
-    middle, up_out, down_out, lower, upper, pair_tab,
-    in_sem, y_send, y_recv, ask_send, ask_recv, x_send, x_recv, halo_send, halo_recv, ready,
+    middle, up_out, down_out, lower, upper, passing, pair_tab,
+    in_sem, y_send, y_recv, ask_send, ask_recv, x_send, x_recv, halo_send, halo_recv,
+    pass_send, pass_recv, on_send, ready,
 ):
     blk, band = lax.axis_index("blk"), lax.axis_index("band")
     bands = lax.axis_size("band")
     half_bands = bands // 2
     y, x = blk // NX, blk % NX
     above, below = (band + 1) % bands, (band + bands - 1) % bands
-    is_first, is_last = band % half_bands == 0, band % half_bands == half_bands - 1
+    place = band % half_bands
+    is_first, is_last = place == 0, place == half_bands - 1
+    far = half_bands >= 4
+    is_patient, is_passer = place == half_bands - 2, place == half_bands - 3
     lane = lax.broadcasted_iota(jnp.int32, (B, 2 * B), 1)
     first_half = lane < B
 
@@ -74,6 +79,14 @@
     @pl.when(is_first)
     def _():
         signal(barrier, (blk, below))
+        if far:
+            signal(barrier, (blk, (band + bands - 3) % bands))
+
+    if far:
+
+        @pl.when(is_passer)
+        def _():
+            signal(barrier, (blk, band + 2))
 
     for copy in inputs[0:2]:
         copy.wait()
@@ -106,7 +119,8 @@
     pl.semaphore_wait(
         barrier,
         NX - 1 + jnp.where(y < NY - 1, 1, 0) + jnp.where(y > 0, 1, 0)
-        + jnp.where(is_first, 0, 1) + jnp.where(is_last, 1, 0),
+        + jnp.where(is_first, 0, 1) + jnp.where(is_last, 2 if far else 1, 0)
+        + (jnp.where(is_passer, 1, 0) if far else 0),
     )
 
     def y_copy(source, target, sender):
@@ -149,6 +163,18 @@
             src_ref=(down_out if side else up_out).at[step], dst_ref=(upper if side else lower).at[step],
             send_sem=halo_send.at[side, step], recv_sem=halo_recv.at[side, step],
             device_id=(blk, below if side else above), device_id_type=MESH,
+        )
+
+    def pass_copy(step, n):
+        return pltpu.make_async_remote_copy(
+            src_ref=up_out.at[step], dst_ref=passing.at[n], send_sem=pass_send.at[n], recv_sem=pass_recv.at[n],
+            device_id=(blk, (band + bands - 2) % bands), device_id_type=MESH,
+        )
+
+    def on_copy(step, n):
+        return pltpu.make_async_remote_copy(
+            src_ref=passing.at[n], dst_ref=lower.at[step], send_sem=on_send.at[n], recv_sem=halo_recv.at[0, step],
+            device_id=(blk, (band + 3) % bands), device_id_type=MESH,
         )
 
     order = [
@@ -214,6 +240,20 @@
         for shift in range(1, NX):
             x_landing(order[turn], shift).wait_recv()
 
+    @pl.when(jnp.logical_not(is_first))
+    def _():
+        signal(ready.at[0], (blk, below))
+
+    @pl.when(is_last)
+    def _():
+        signal(ready.at[1], (blk, above))
+
+    if far:
+
+        @pl.when(is_patient)
+        def _():
+            pl.semaphore_wait(ready.at[2], 1)
+
     @pl.when(y < NY - 1)
     def _():
         y_copy(y, y + 1, 0).start()
@@ -224,14 +264,6 @@
 
     for shift in (2, 1, 3):
         ask_copy(shift).start()
-
-    @pl.when(jnp.logical_not(is_first))
-    def _():
-        signal(ready.at[0], (blk, below))
-
-    @pl.when(is_last)
-    def _():
-        signal(ready.at[1], (blk, above))
 
     def windowed(values, code, at_code):
         chosen = jnp.where(code == at_code, values, 0.0)
@@ -290,8 +322,41 @@
         middle[step] = total[B : 2 * B]
         up_out[step] = total[2 * B : 3 * B]
 
-    def send_up(step):
-        halo_copy(step, 0).start()
+    def send_up(turn):
+        def start(n, direct):
+            step = 2 * order[turn] + n
+            if direct:
+                halo_copy(step, 0).start()
+            else:
+                pass_copy(step, 2 * turn + n).start()
+
+        up_either(turn, start)
+
+    def up_either(turn, act):
+        if far and 2 * turn < DETOURS:
+
+            @pl.when(is_last)
+            def _():
+                act(0, False)
+                act(1, False)
+
+            @pl.when(jnp.logical_not(is_last))
+            def _():
+                act(0, True)
+                act(1, True)
+        else:
+            act(0, True)
+            act(1, True)
+
+    def pass_on(turn):
+        if far:
+
+            @pl.when(is_passer)
+            def _():
+                for n in range(2):
+                    step = 2 * order[turn] + n
+                    pass_copy(step, 2 * turn + n).wait_recv()
+                    on_copy(step, 2 * turn + n).start()
 
     def send_down(step):
         halo_copy(step, 1).start()
@@ -330,7 +395,8 @@
     def _():
         pl.semaphore_wait(ready.at[0], 1)
 
-    both_steps(0, compute, send_up)
+    both_steps(0, compute)
+    send_up(0)
 
     @pl.when(jnp.logical_not(is_first))
     def _():
@@ -338,7 +404,8 @@
 
     y_take(3)
     x_take(1)
-    both_steps(1, compute, send_up)
+    both_steps(1, compute)
+    send_up(1)
 
     @pl.when(is_first)
     def _():
@@ -346,10 +413,22 @@
         both_steps(0, send_down)
 
     both_steps(1, send_down)
+    pass_on(0)
     x_take(2)
-    both_steps(2, compute, send_up, send_down)
+    both_steps(2, compute)
+    send_up(2)
+    both_steps(2, send_down)
+    pass_on(1)
     x_take(3)
-    both_steps(3, compute, send_up, send_down)
+    if far:
+
+        @pl.when(is_last)
+        def _():
+            signal(ready.at[2], (blk, below))
+
+    both_steps(3, compute)
+    send_up(3)
+    both_steps(3, send_down)
     for turn in range(4):
         both_steps(turn, finish)
 
@@ -379,11 +458,26 @@
     lax.fori_loop(0, NY, drain_x, 0)
 
     def drain_halo(step, carry):
-        halo_copy(step, 0).wait_send()
         halo_copy(step, 1).wait_send()
         return carry
 
     lax.fori_loop(0, STEPS, drain_halo, 0)
+    for turn in range(4):
+
+        def drain_up(n, direct, turn=turn):
+            step = 2 * order[turn] + n
+            if direct:
+                halo_copy(step, 0).wait_send()
+            else:
+                pass_copy(step, 2 * turn + n).wait_send()
+
+        up_either(turn, drain_up)
+    if far:
+
+        @pl.when(is_passer)
+        def _():
+            for n in range(DETOURS):
+                on_copy(2 * order[n // 2] + n % 2, n).wait_send()
 
 
 def body(fine_blocks, source_group, source_row, prolong_blocks, prolong_code):
@@ -411,13 +505,15 @@
             pltpu.VMEM((2 * MB * B, window), BF16),
             pltpu.VMEM((2 * MB * B, window), BF16),
             halo, halo, halo, halo, halo,
+            pltpu.VMEM((DETOURS, B, window), F32),
             pltpu.SMEM((MB * NX * NY,), jnp.int32),
             dma((5,)),
             dma((5,)), dma((NY,)),
             dma((NX,)), dma((NX,)),
             dma((NX, NY)), dma((NX, NY)),
             dma((2, STEPS)), dma((2, STEPS)),
-            pltpu.SemaphoreType.REGULAR((2,)),
+            dma((DETOURS,)), dma((DETOURS,)), dma((DETOURS,)),
+            pltpu.SemaphoreType.REGULAR((3,)),
         ],
         compiler_params=pltpu.CompilerParams(
             collective_id=0, has_side_effects=True, vmem_limit_bytes=60 * 2**20

time: 49.9 us -> 50.6 us (1.014)
  the two profiles are of different devices: /device:TPU:8 before, /device:TPU:385 now
where the time goes in v3:
time: 50.6 us; the launch traced here: 50.5 us
  Pallas kernels  48 us (95%)
  local copies, waits for them, and re-layouts  2.47 us (5%)
    pallas_call x1, Pallas kernels, body(): pl.pallas_call(kernel, out_shape=jax.ShapeDtypeStruct((B, 5 * NX * NY * B...  48 us
    unnamed x1, local copies, waits for them, and re-layouts  2.47 us

profile of v3, /device:TPU:385, one launch (start us, length us, event | category | flops | bytes accessed | tf_op | source)
XLA Modules:
  0.0 50.5 jit_solution(17173639266640490134)
XLA Ops:
  0.0 48.0 %galerkin.1 = f32[64,5120]{1,0:T(8,128)} custom-call(f32[4,64,256]{2,1,0:T(8,128)} %a_hbm.1, f32[256,128]{1,0:T(8,128)} %bitcast.2, s32[4,4]{1,0:T(4,128)} %group_hbm.1, s32[4,4]{1,0:T(4,128)} %row_hbm.1, s32[2,4]{1,0:T(2,128)} %bitcast.3), custom_call_target="tpu_custom_call" | custom-call | flops 1000000000 | bytes 4194304 | tf_op jit(solution)/shard_map/galerkin/pallas_call | solution.py:488
  48.0 2.5 %copy.7 = f32[64,5120]{1,0:T(8,128)} copy(f32[64,5120]{1,0:T(8,128)} %galerkin.1) | data formatting | bytes 2621440

commit v4 on v3

--- a/solution.py
+++ b/solution.py
@@ -44,6 +44,9 @@
     def at(row, column):
         return (row * NX + column, band)
 
+    def inside(row):
+        return (row >= 0) & (row < NY)
+
     def beside(shift):
         return (x + shift) % NX
 
@@ -64,13 +67,11 @@
     for shift in range(1, NX):
         signal(barrier, at(y, beside(shift)))
 
-    @pl.when(y < NY - 1)
-    def _():
-        signal(barrier, at(y + 1, x))
-
-    @pl.when(y > 0)
-    def _():
-        signal(barrier, at(y - 1, x))
+    for jump in (1, -1, 2, -2):
+
+        @pl.when(inside(y + jump))
+        def _():
+            signal(barrier, at(y + jump, x))
 
     @pl.when(jnp.logical_not(is_last))
     def _():
@@ -118,7 +119,7 @@
 
     pl.semaphore_wait(
         barrier,
-        NX - 1 + jnp.where(y < NY - 1, 1, 0) + jnp.where(y > 0, 1, 0)
+        NX - 1 + sum(jnp.where(inside(y + jump), 1, 0) for jump in (1, -1, 2, -2))
         + jnp.where(is_first, 0, 1) + jnp.where(is_last, 2 if far else 1, 0)
         + (jnp.where(is_passer, 1, 0) if far else 0),
     )
@@ -184,11 +185,11 @@
         jnp.where(y < 2, 3, 0),
     ]
 
-    def onward(source):
-        return jnp.where(source < y, y + 1, y - 1)
-
-    def inside(target):
-        return (target >= 0) & (target < NY)
+    def hands_on(source):
+        return ((y == 2) & (source == 0)) | ((y == 1) & (source == 3))
+
+    hand_target = jnp.where(y == 2, 3, 0)
+    is_end = (y == 0) | (y == NY - 1)
 
     def serve(turn):
         source = order[turn]
@@ -227,14 +228,11 @@
 
     def y_take(turn):
         source = order[turn]
-        y_copy(source, jnp.where(source < y, y - 1, y + 1), 1 + turn).wait_recv()
-        target = onward(source)
-
-        @pl.when(inside(target))
-        def _():
-            y_copy(source, target, 1 + turn).start()
-
-        serve(turn)
+        y_copy(source, jnp.where(source < y, y - 1, y + 1), 0).wait_recv()
+
+        @pl.when(hands_on(source))
+        def _():
+            y_copy(source, hand_target, 4).start()
 
     def x_take(turn):
         for shift in range(1, NX):
@@ -248,19 +246,11 @@
     def _():
         signal(ready.at[1], (blk, above))
 
-    if far:
-
-        @pl.when(is_patient)
-        def _():
-            pl.semaphore_wait(ready.at[2], 1)
-
-    @pl.when(y < NY - 1)
-    def _():
-        y_copy(y, y + 1, 0).start()
-
-    @pl.when(y > 0)
-    def _():
-        y_copy(y, y - 1, 1).start()
+    for n, jump in enumerate((1, -1, 2, -2)):
+
+        @pl.when(inside(y + jump))
+        def _():
+            y_copy(y, y + jump, n).start()
 
     for shift in (2, 1, 3):
         ask_copy(shift).start()
@@ -322,31 +312,32 @@
         middle[step] = total[B : 2 * B]
         up_out[step] = total[2 * B : 3 * B]
 
-    def send_up(turn):
+    def send_up(turn, n):
+        step = 2 * order[turn] + n
+
         def start(n, direct):
-            step = 2 * order[turn] + n
             if direct:
                 halo_copy(step, 0).start()
             else:
                 pass_copy(step, 2 * turn + n).start()
 
-        up_either(turn, start)
-
-    def up_either(turn, act):
+        up_either(turn, start, (n,))
+
+    def up_either(turn, act, which):
         if far and 2 * turn < DETOURS:
 
             @pl.when(is_last)
             def _():
-                act(0, False)
-                act(1, False)
+                for n in which:
+                    act(n, False)
 
             @pl.when(jnp.logical_not(is_last))
             def _():
-                act(0, True)
-                act(1, True)
+                for n in which:
+                    act(n, True)
         else:
-            act(0, True)
-            act(1, True)
+            for n in which:
+                act(n, True)
 
     def pass_on(turn):
         if far:
@@ -372,80 +363,98 @@
             column = pl.multiple_of(e * NX * NY * B + step * 2 * B, 2 * B)
             out_ref[:, pl.ds(column, 2 * B)] = sum(parts[1:], parts[0])
 
-    def both_steps(turn, *work):
+    def both_steps(turn, work):
         def one(n, carry):
-            for each in work:
-                each(2 * order[turn] + n)
+            work(2 * order[turn] + n)
             return carry
 
         lax.fori_loop(0, 2, one, 0)
+
+    def multiply(turn):
+        def one(n, carry):
+            step = 2 * order[turn] + n
+            compute(step)
+            send_up(turn, n)
+            if turn == 0:
+
+                @pl.when(jnp.logical_not(is_first))
+                def _():
+                    send_down(step)
+            else:
+                send_down(step)
+            return carry
+
+        lax.fori_loop(0, 2, one, 0)
+
+    def unless_patient(condition, turn):
+        if far:
+            condition = condition & jnp.logical_not(is_patient)
+
+        @pl.when(condition)
+        def _():
+            y_take(turn)
 
     inputs[4].wait()
     lax.fori_loop(0, 2, left_product, 0)
     for shift in range(1, NX):
         ask_landing(shift).wait_recv()
+    if far:
+
+        @pl.when(is_patient)
+        def _():
+            for turn in range(1, 4):
+                y_take(turn)
+            pl.semaphore_wait(ready.at[2], 1)
+
     serve(0)
     lax.fori_loop(2, 3, left_product, 0)
-    y_take(1)
+    unless_patient(y >= 0, 1)
+    serve(1)
     lax.fori_loop(3, 4, left_product, 0)
-    y_take(2)
+    unless_patient(y >= 0, 2)
+    serve(2)
+    unless_patient(jnp.logical_not(is_end), 3)
     x_take(0)
 
     @pl.when(jnp.logical_not(is_last))
     def _():
         pl.semaphore_wait(ready.at[0], 1)
 
-    both_steps(0, compute)
-    send_up(0)
-
-    @pl.when(jnp.logical_not(is_first))
-    def _():
-        both_steps(0, send_down)
-
-    y_take(3)
+    multiply(0)
+    unless_patient(is_end, 3)
+    serve(3)
+    if far:
+
+        @pl.when(is_last)
+        def _():
+            signal(ready.at[2], (blk, below))
+
     x_take(1)
-    both_steps(1, compute)
-    send_up(1)
 
     @pl.when(is_first)
     def _():
         pl.semaphore_wait(ready.at[1], 1)
         both_steps(0, send_down)
 
-    both_steps(1, send_down)
+    multiply(1)
     pass_on(0)
     x_take(2)
-    both_steps(2, compute)
-    send_up(2)
-    both_steps(2, send_down)
+    multiply(2)
     pass_on(1)
     x_take(3)
-    if far:
-
-        @pl.when(is_last)
-        def _():
-            signal(ready.at[2], (blk, below))
-
-    both_steps(3, compute)
-    send_up(3)
-    both_steps(3, send_down)
+    multiply(3)
     for turn in range(4):
         both_steps(turn, finish)
 
-    @pl.when(y < NY - 1)
-    def _():
-        y_copy(y, y + 1, 0).wait_send()
-
-    @pl.when(y > 0)
-    def _():
-        y_copy(y, y - 1, 1).wait_send()
-
-    for turn in range(1, 4):
-        target = onward(order[turn])
-
-        @pl.when(inside(target))
-        def _():
-            y_copy(order[turn], target, 1 + turn).wait_send()
+    for n, jump in enumerate((1, -1, 2, -2)):
+
+        @pl.when(inside(y + jump))
+        def _():
+            y_copy(y, y + jump, n).wait_send()
+
+    @pl.when(jnp.logical_not(is_end))
+    def _():
+        y_copy(3 - hand_target, hand_target, 4).wait_send()
 
     for shift in range(1, NX):
         ask_copy(shift).wait_send()
@@ -471,7 +480,7 @@
             else:
                 pass_copy(step, 2 * turn + n).wait_send()
 
-        up_either(turn, drain_up)
+        up_either(turn, drain_up, (0, 1))
     if far:
 
         @pl.when(is_passer)
@@ -516,11 +525,14 @@
             pltpu.SemaphoreType.REGULAR((3,)),
         ],
         compiler_params=pltpu.CompilerParams(
-            collective_id=0, has_side_effects=True, vmem_limit_bytes=60 * 2**20
+            collective_id=0, has_side_effects=True, vmem_limit_bytes=40 * 2**20
         ),
         cost_estimate=pl.CostEstimate(flops=10**9, bytes_accessed=4 * 2**20, transcendentals=0),
         name="galerkin",
-    )(fine_blocks, prolong_blocks.reshape(FB * B, 2 * B), source_group, source_row, prolong_code.T)
+    )(*[
+        pltpu.with_memory_space_constraint(each, pltpu.HBM)
+        for each in (fine_blocks, prolong_blocks.reshape(FB * B, 2 * B), source_group, source_row, prolong_code.T)
+    ])
 
 
 def solution(mesh):

time: 50.6 us -> 44.4 us (0.88)
  the two profiles are of different devices: /device:TPU:385 before, /device:TPU:36 now
where the time goes in v4:
time: 44.4 us; the launch traced here: 44.3 us
  Pallas kernels  43.2 us (97%)
  local copies, waits for them, and re-layouts  1.06 us (2%)
    pallas_call x1, Pallas kernels, body(): pl.pallas_call(kernel, out_shape=jax.ShapeDtypeStruct((B, 5 * NX * NY * B...  43.2 us
    unnamed x1, local copies, waits for them, and re-layouts  1.06 us

profile of v4, /device:TPU:36, one launch (start us, length us, event | category | flops | bytes accessed | tf_op | source)
XLA Modules:
  0.0 44.3 jit_solution(5507741551900207544)
XLA Ops:
  0.0 43.2 %galerkin.1 = f32[64,5120]{1,0:T(8,128)S(1)} custom-call(f32[4,64,256]{2,1,0:T(8,128)} %a_hbm.1, f32[256,128]{1,0:T(8,128)} %bitcast.2, s32[4,4]{1,0:T(4,128)} %group_hbm.1, s32[4,4]{1,0:T(4,128)} %row_hbm.1, s32[2,4]{1,0:T(2,128)} %bitcast.3), custom_call_target="tpu_custom_call" | custom-call | flops 1000000000 | bytes 4194304 | tf_op jit(solution)/shard_map/galerkin/pallas_call | solution.py:497
  43.3 1.1 %copy.7 = f32[64,5120]{1,0:T(8,128)} copy(f32[64,5120]{1,0:T(8,128)S(1)} %galerkin.1) | data formatting | bytes 2621440

commit v5 on v4

v5 whole, which is shorter than its diff:
```python
import jax
import jax.numpy as jnp
from jax import lax
from jax.experimental import pallas as pl
from jax.experimental.pallas import tpu as pltpu
from jax.sharding import PartitionSpec as P

MESH = pl.DeviceIdType.MESH
F32 = jnp.float32
BF16 = jnp.bfloat16

B = 64
FB = 4
KA = 4
MB = 2
NX = 4
NY = 4
PACK = FB * B + 8
SHARE = MB * B + 8
STEPS = NX * NY // 2
DETOURS = (4, 2)
HEAD = 136


def kernel(
    a_hbm, p_hbm, group_hbm, row_hbm, code_hbm, out_ref,
    a_ref, group_ref, row_ref, code_ref,
    held, want, asked, staged, got, left_hi, left_lo, win_hi, win_lo,
    middle, up_out, down_out, lower, upper, passing, pair_tab,
    in_sem, y_send, y_recv, ask_send, ask_recv, x_send, x_recv, halo_send, halo_recv,
    pass_send, pass_recv, on_send, ready,
):
    blk, band = lax.axis_index("blk"), lax.axis_index("band")
    bands = lax.axis_size("band")
    half_bands = bands // 2
    y, x = blk // NX, blk % NX
    above, below = (band + 1) % bands, (band + bands - 1) % bands
    place = band % half_bands
    is_first, is_last = place == 0, place == half_bands - 1
    far = half_bands >= 4
    is_patient, is_passer = place == half_bands - 2, (place == half_bands - 3, place == 2)
    lane = lax.broadcasted_iota(jnp.int32, (B, 2 * B), 1)
    first_half = lane < B

    def at(row, column):
        return (row * NX + column, band)

    def inside(row):
        return (row >= 0) & (row < NY)

    def beside(shift):
        return (x + shift) % NX

    def signal(semaphore, target):
        pl.semaphore_signal(semaphore, inc=1, device_id=target, device_id_type=MESH)

    inputs = [
        pltpu.make_async_copy(source, target, in_sem.at[n])
        for n, (source, target) in enumerate((
            (group_hbm, group_ref), (row_hbm, row_ref), (code_hbm, code_ref),
            (p_hbm, held.at[y, pl.ds(0, FB * B)]), (a_hbm, a_ref),
        ))
    ]
    for copy in inputs:
        copy.start()

    barrier = pltpu.get_barrier_semaphore()
    for shift in range(1, NX):
        signal(barrier, at(y, beside(shift)))

    for jump in (1, -1, 2, -2):

        @pl.when(inside(y + jump))
        def _():
            signal(barrier, at(y + jump, x))

    @pl.when(jnp.logical_not(is_last))
    def _():
        signal(barrier, (blk, above))

    @pl.when(is_first)
    def _():
        signal(barrier, (blk, below))
        if far:
            signal(barrier, (blk, (band + bands - 3) % bands))
            signal(barrier, (blk, band + 2))

    if far:

        @pl.when(is_passer[0])
        def _():
            signal(barrier, (blk, band + 2))

        @pl.when(is_passer[1])
        def _():
            signal(barrier, (blk, (band + bands - 3) % bands))

    inputs[2].wait()
    tile_row = lax.broadcasted_iota(jnp.int32, (8, 2 * B), 0)
    tile_lane = lax.broadcasted_iota(jnp.int32, (8, 2 * B), 1)
    codes = jnp.zeros((8, 2 * B), F32)
    for i in range(FB):
        one = jnp.where(tile_lane < B, code_ref[0, i], code_ref[1, i]).astype(F32)
        codes = jnp.where(tile_row == i, one, codes)
    held[y, FB * B : PACK, :] = codes
    inputs[3].wait()

    pl.semaphore_wait(
        barrier,
        NX - 1 + sum(jnp.where(inside(y + jump), 1, 0) for jump in (1, -1, 2, -2))
        + jnp.where(is_first, 0, 1) + jnp.where(is_last, 3 if far else 1, 0)
        + (jnp.where(is_passer[0] | is_passer[1], 1, 0) if far else 0),
    )

    def y_copy(source, target, sender, part=None):
        rows = pl.ds(0, PACK) if part is None else (pl.ds(0, HEAD), pl.ds(HEAD, PACK - HEAD))[part]
        slot = held.at[source, rows]
        return pltpu.make_async_remote_copy(
            src_ref=slot, dst_ref=slot, send_sem=y_send.at[sender], recv_sem=y_recv.at[part or 0, source],
            device_id=at(target, x), device_id_type=MESH,
        )

    def ask_copy(shift):
        return pltpu.make_async_remote_copy(
            src_ref=want.at[beside(shift)], dst_ref=asked.at[NX - shift],
            send_sem=ask_send.at[shift], recv_sem=ask_recv.at[NX - shift],
            device_id=at(y, beside(shift)), device_id_type=MESH,
        )

    def x_copy(source, shift):
        return pltpu.make_async_remote_copy(
            src_ref=staged.at[shift, source], dst_ref=got.at[x, source],
            send_sem=x_send.at[shift, source], recv_sem=x_recv.at[shift, source],
            device_id=at(y, beside(shift)), device_id_type=MESH,
        )

    def x_landing(source, shift):
        return pltpu.make_async_remote_copy(
            src_ref=staged.at[shift, source], dst_ref=got.at[beside(NX - shift), source],
            send_sem=x_send.at[shift, source], recv_sem=x_recv.at[shift, source],
            device_id=at(y, beside(shift)), device_id_type=MESH,
        )

    def ask_landing(shift):
        return pltpu.make_async_remote_copy(
            src_ref=want.at[beside(shift)], dst_ref=asked.at[shift],
            send_sem=ask_send.at[shift], recv_sem=ask_recv.at[shift],
            device_id=at(y, beside(shift)), device_id_type=MESH,
        )

    def halo_copy(step, side):
        return pltpu.make_async_remote_copy(
            src_ref=(down_out if side else up_out).at[step], dst_ref=(upper if side else lower).at[step],
            send_sem=halo_send.at[side, step], recv_sem=halo_recv.at[side, step],
            device_id=(blk, below if side else above), device_id_type=MESH,
        )

    def pass_copy(side, step, n):
        return pltpu.make_async_remote_copy(
            src_ref=(down_out if side else up_out).at[step], dst_ref=passing.at[side, n],
            send_sem=pass_send.at[side, n], recv_sem=pass_recv.at[side, n],
            device_id=(blk, (band + (2 if side else bands - 2)) % bands), device_id_type=MESH,
        )

    def on_copy(side, step, n):
        return pltpu.make_async_remote_copy(
            src_ref=passing.at[side, n], dst_ref=(upper if side else lower).at[step],
            send_sem=on_send.at[side, n], recv_sem=halo_recv.at[side, step],
            device_id=(blk, (band + (bands - 3 if side else 3)) % bands), device_id_type=MESH,
        )

    order = [
        y,
        jnp.where(y == 0, 1, y - 1),
        jnp.where(y == 0, 2, jnp.where(y == 3, 1, y + 1)),
        jnp.where(y < 2, 3, 0),
    ]

    is_end = (y == 0) | (y == NY - 1)
    end_jump = jnp.where(y == 0, 1, -1)
    inner_jump = jnp.where(y == 1, 1, -1)
    hand_source, hand_target = jnp.where(y == 1, 3, 0), jnp.where(y == 1, 0, 3)

    def y_sends(act):
        @pl.when(is_end)
        def _():
            act(y_copy(y, y + 2 * end_jump, 0, 0))
            act(y_copy(y, y + 2 * end_jump, 1, 1))
            act(y_copy(y, y + end_jump, 2))

        @pl.when(jnp.logical_not(is_end))
        def _():
            act(y_copy(y, y + inner_jump, 2))
            act(y_copy(y, y - inner_jump, 3))
            act(y_copy(y, y + 2 * inner_jump, 0))

    def hand_on(part):
        return y_copy(hand_source, hand_target, 4 + part, part)

    def serve(turn):
        source = order[turn]

        def choose(wanted, slot, target):
            row = wanted(MB * source + slot)
            pick = jnp.broadcast_to(row, (B, 2 * B))
            values = jnp.zeros((B, 2 * B), F32)
            code = jnp.zeros((1, 2 * B), F32)
            for i in range(FB):
                values = jnp.where(pick == i, held[source, i * B : (i + 1) * B, :], values)
                code = jnp.where(row == i, held[source, FB * B + i : FB * B + i + 1, :], code)
            target(slice(slot * B, (slot + 1) * B), values)
            target(slice(MB * B + slot, MB * B + slot + 1), code)

        for shift in (2, 1, 3):
            for slot in range(MB):

                def wanted(n, shift=shift):
                    return asked[shift, pl.ds(n, 1), :]

                def target(rows, values, shift=shift):
                    staged[shift, source, rows, :] = values

                choose(wanted, slot, target)
            x_copy(source, shift).start()
        for slot in range(MB):

            def own(n):
                return want[x, pl.ds(n, 1), :]

            def keep(rows, values):
                got[x, source, rows, :] = values

            choose(own, slot, keep)

    def y_take(turn):
        source = order[turn]
        sender = jnp.where(source < y, y - 1, y + 1)
        if turn < 3:
            y_copy(source, sender, 0).wait_recv()
            return
        for part in range(2):
            y_copy(source, sender, 0, part).wait_recv()

            @pl.when(jnp.logical_not(is_end))
            def _():
                hand_on(part).start()

    def x_take(turn):
        for shift in range(1, NX):
            x_landing(order[turn], shift).wait_recv()

    @pl.when(jnp.logical_not(is_first))
    def _():
        signal(ready.at[0], (blk, below))

    @pl.when(is_last)
    def _():
        signal(ready.at[1], (blk, above))
        if far:
            signal(ready.at[4], (blk, (band + 3) % bands))

    if far:

        @pl.when(is_passer[1])
        def _():
            signal(ready.at[3], (blk, band - 2))

        @pl.when(is_patient)
        def _():
            pl.semaphore_wait(ready.at[2], 1)

    y_sends(lambda copy: copy.start())

    for copy in inputs[0:2]:
        copy.wait()

    def tabulate(group, carry):
        pair = [jnp.int32(0), jnp.int32(0)]
        row = [jnp.int32(FB), jnp.int32(FB)]
        for at_pair in range(FB * KA - 1, -1, -1):
            i, k = at_pair // KA, at_pair % KA
            hit = group_ref[i, k] == group
            pair = [jnp.where(hit, at_pair, pair[0]), jnp.where(hit, pair[0], pair[1])]
            row = [jnp.where(hit, row_ref[i, k], row[0]), jnp.where(hit, row[0], row[1])]
        for slot in range(MB):
            pair_tab[MB * group + slot] = pair[slot]
            want[group % NX, pl.ds(MB * (group // NX) + slot, 1), :] = jnp.full((1, 2 * B), row[slot]).astype(F32)
        return carry

    lax.fori_loop(0, NX * NY, tabulate, 0)

    for shift in (2, 1, 3):
        ask_copy(shift).start()

    def windowed(values, code, at_code):
        chosen = jnp.where(code == at_code, values, 0.0)
        return chosen + pltpu.roll(chosen, B, 1)

    def left_product(i, carry):
        p_here = held[y, pl.ds(pl.multiple_of(i * B, B), B), :]
        code = jnp.broadcast_to(held[y, pl.ds(FB * B + i, 1), :], (B, 2 * B))
        parts = [windowed(p_here, code, d) for d in range(3)]
        restrict = jnp.concatenate(
            [jnp.where(first_half, parts[0], parts[1]), jnp.where(first_half, parts[2], 0.0)], axis=1
        )
        twice = []
        for side in range(2):
            both = a_ref[i, :, side * 2 * B : (side + 1) * 2 * B]
            turned = pltpu.roll(both, B, 1)
            twice += [jnp.where(first_half, both, turned), jnp.where(first_half, turned, both)]
        result = lax.dot_general(
            restrict, jnp.concatenate(twice, axis=1), (((0,), (0,)), ((), ())),
            precision=lax.Precision.HIGHEST, preferred_element_type=F32,
        )[0 : 3 * B]
        high = result.astype(BF16)
        low = (result - high.astype(F32)).astype(BF16)
        for k in range(KA):
            left_hi[i * KA + k] = high[:, k * 2 * B : (k + 1) * 2 * B]
            left_lo[i * KA + k] = low[:, k * 2 * B : (k + 1) * 2 * B]
        return carry

    wide_half = lax.broadcasted_iota(jnp.int32, (3 * B, 2 * B), 1) < B

    def compute(step):
        for half in range(2):
            row, column = step // 2, 2 * (step % 2) + half
            for slot in range(MB):
                values = got[column, row, slot * B : (slot + 1) * B, :]
                code = jnp.broadcast_to(got[column, row, MB * B + slot : MB * B + slot + 1, :], (B, 2 * B))
                mine = first_half if half == 0 else jnp.logical_not(first_half)
                at_row = (MB * half + slot) * B
                for e in range(3):
                    part = jnp.where(mine, windowed(values, code, e), 0.0)
                    high = part.astype(BF16)
                    win_hi[at_row : at_row + B, e * 2 * B : (e + 1) * 2 * B] = high
                    win_lo[at_row : at_row + B, e * 2 * B : (e + 1) * 2 * B] = (part - high.astype(F32)).astype(BF16)

        def stacked(ref):
            pairs = [ref[pair_tab[2 * MB * step + n]] for n in range(2 * MB)]
            return jnp.concatenate(
                [jnp.where(wide_half, pairs[0], pairs[1]), jnp.where(wide_half, pairs[2], pairs[3])], axis=1
            )

        high, low = stacked(left_hi), stacked(left_lo)
        total = jnp.dot(high, win_hi[...], preferred_element_type=F32)
        total += jnp.dot(high, win_lo[...], preferred_element_type=F32)
        total += jnp.dot(low, win_hi[...], preferred_element_type=F32)
        down_out[step] = total[0:B]
        middle[step] = total[B : 2 * B]
        up_out[step] = total[2 * B : 3 * B]

    def detour(side, turn, n):
        if side == 0:
            return is_last & (n == 1), turn
        return is_first & (turn == 0), n

    def each_way(side, turn, n, act):
        step = 2 * order[turn] + n
        if not far or (side and turn):
            act(halo_copy(step, side))
            return
        around, index = detour(side, turn, n)

        @pl.when(around)
        def _():
            act(pass_copy(side, step, index))

        @pl.when(jnp.logical_not(around))
        def _():
            act(halo_copy(step, side))

    def passed_on(side, turn):
        return [(2 * order[turn] + 1, turn)] if side == 0 else [(2 * order[turn] + n, n) for n in range(2 - 2 * min(turn, 1))]

    def pass_on(turn):
        for side in range(2):
            if far and passed_on(side, turn):

                @pl.when(is_passer[side])
                def _():
                    if side:
                        pl.semaphore_wait(ready.at[4], 1)
                    for step, index in passed_on(side, turn):
                        pass_copy(side, step, index).wait_recv()
                        on_copy(side, step, index).start()

    def finish(step):
        halo_copy(step, 0).wait_recv()
        halo_copy(step, 1).wait_recv()
        for e in range(5):
            parts = []
            for ref, shift in ((lower, 0), (middle, 1), (upper, 2)):
                if 0 <= e - shift < 3:
                    parts.append(ref[step, :, (e - shift) * 2 * B : (e - shift + 1) * 2 * B])
            column = pl.multiple_of(e * NX * NY * B + step * 2 * B, 2 * B)
            out_ref[:, pl.ds(column, 2 * B)] = sum(parts[1:], parts[0])

    def both_steps(turn, work):
        def one(n, carry):
            work(2 * order[turn] + n)
            return carry

        lax.fori_loop(0, 2, one, 0)

    def multiply(turn):
        def one(n, carry):
            compute(2 * order[turn] + n)
            for side in range(2):
                each_way(side, turn, n, lambda copy: copy.start())
            return carry

        lax.fori_loop(0, 2, one, 0)

    inputs[4].wait()
    lax.fori_loop(0, 2, left_product, 0)
    for shift in range(1, NX):
        ask_landing(shift).wait_recv()
    serve(0)
    lax.fori_loop(2, 3, left_product, 0)
    y_take(1)
    serve(1)
    lax.fori_loop(3, 4, left_product, 0)
    y_take(2)
    serve(2)

    @pl.when(jnp.logical_not(is_end))
    def _():
        y_take(3)

    x_take(0)

    @pl.when(jnp.logical_not(is_last))
    def _():
        pl.semaphore_wait(ready.at[0], 1)

    @pl.when(is_first)
    def _():
        pl.semaphore_wait(ready.at[3 if far else 1], 1)

    multiply(0)

    @pl.when(is_end)
    def _():
        y_take(3)

    if far:

        @pl.when(is_last)
        def _():
            signal(ready.at[2], (blk, below))

    serve(3)
    x_take(1)
    if far:

        @pl.when(is_first)
        def _():
            pl.semaphore_wait(ready.at[1], 1)

    multiply(1)
    pass_on(0)
    x_take(2)
    multiply(2)
    pass_on(1)
    x_take(3)
    multiply(3)
    pass_on(2)
    pass_on(3)
    for turn in range(4):
        both_steps(turn, finish)

    y_sends(lambda copy: copy.wait_send())

    @pl.when(jnp.logical_not(is_end))
    def _():
        hand_on(0).wait_send()
        hand_on(1).wait_send()

    for shift in range(1, NX):
        ask_copy(shift).wait_send()

    def drain_x(source, carry):
        for shift in range(1, NX):
            x_copy(source, shift).wait_send()
        return carry

    lax.fori_loop(0, NY, drain_x, 0)

    for side in range(2):
        for turn in range(4):
            for n in range(2):
                each_way(side, turn, n, lambda copy: copy.wait_send())
            if far and passed_on(side, turn):

                @pl.when(is_passer[side])
                def _():
                    for step, index in passed_on(side, turn):
                        on_copy(side, step, index).wait_send()


def body(fine_blocks, source_group, source_row, prolong_blocks, prolong_code):
    hbm = pl.BlockSpec(memory_space=pltpu.HBM)
    window = 3 * 2 * B
    halo = pltpu.VMEM((STEPS, B, window), F32)
    dma = pltpu.SemaphoreType.DMA
    return pl.pallas_call(
        kernel,
        out_shape=jax.ShapeDtypeStruct((B, 5 * NX * NY * B), F32),
        in_specs=[hbm] * 5,
        out_specs=pl.BlockSpec(memory_space=pltpu.VMEM),
        scratch_shapes=[
            pltpu.VMEM((FB, B, KA * B), F32),
            pltpu.SMEM((FB, KA), jnp.int32),
            pltpu.SMEM((FB, KA), jnp.int32),
            pltpu.SMEM((2, FB), jnp.int32),
            pltpu.VMEM((NY, PACK, 2 * B), F32),
            pltpu.VMEM((NX, NY * MB, 2 * B), F32),
            pltpu.VMEM((NX, NY * MB, 2 * B), F32),
            pltpu.VMEM((NX, NY, SHARE, 2 * B), F32),
            pltpu.VMEM((NX, NY, SHARE, 2 * B), F32),
            pltpu.VMEM((FB * KA, 3 * B, 2 * B), BF16),
            pltpu.VMEM((FB * KA, 3 * B, 2 * B), BF16),
            pltpu.VMEM((2 * MB * B, window), BF16),
            pltpu.VMEM((2 * MB * B, window), BF16),
            halo, halo, halo, halo, halo,
            pltpu.VMEM((2, max(DETOURS), B, window), F32),
            pltpu.SMEM((MB * NX * NY,), jnp.int32),
            dma((5,)),
            dma((6,)), dma((2, NY)),
            dma((NX,)), dma((NX,)),
            dma((NX, NY)), dma((NX, NY)),
            dma((2, STEPS)), dma((2, STEPS)),
            dma((2, max(DETOURS))), dma((2, max(DETOURS))), dma((2, max(DETOURS))),
            pltpu.SemaphoreType.REGULAR((5,)),
        ],
        compiler_params=pltpu.CompilerParams(
            collective_id=0, has_side_effects=True, vmem_limit_bytes=40 * 2**20
        ),
        cost_estimate=pl.CostEstimate(flops=10**9, bytes_accessed=4 * 2**20, transcendentals=0),
        name="galerkin",
    )(*[
        pltpu.with_memory_space_constraint(each, pltpu.HBM)
        for each in (fine_blocks, prolong_blocks.reshape(FB * B, 2 * B), source_group, source_row, prolong_code.T)
    ])


def solution(mesh):
    return jax.shard_map(
        body,
        mesh=mesh,
        in_specs=(
            P(("blk", "band"), None, None),
            P(("blk", "band"), None),
            P(("blk", "band"), None),
            P(("blk", "band"), None, None),
            P(("blk", "band"), None),
        ),
        out_specs=P(("blk", "band"), None),
        check_vma=False,
    )
```

time: 44.4 us -> 42.8 us (0.964)
  the two profiles are of different devices: /device:TPU:36 before, /device:TPU:6 now
where the time goes in v5:
time: 42.8 us; the launch traced here: 42.5 us
  Pallas kernels  41.4 us (97%)
  local copies, waits for them, and re-layouts  1.06 us (2%)
    pallas_call x1, Pallas kernels, body(): pl.pallas_call(kernel, out_shape=jax.ShapeDtypeStruct((B, 5 * NX * NY * B...  41.4 us
    unnamed x1, local copies, waits for them, and re-layouts  1.06 us

profile of v5, /device:TPU:6, one launch (start us, length us, event | category | flops | bytes accessed | tf_op | source)
XLA Modules:
  0.0 42.5 jit_solution(1810786603826907709)
XLA Ops:
  0.0 41.4 %galerkin.1 = f32[64,5120]{1,0:T(8,128)S(1)} custom-call(f32[4,64,256]{2,1,0:T(8,128)} %a_hbm.1, f32[256,128]{1,0:T(8,128)} %bitcast.2, s32[4,4]{1,0:T(4,128)} %group_hbm.1, s32[4,4]{1,0:T(4,128)} %row_hbm.1, s32[2,4]{1,0:T(2,128)} %bitcast.3), custom_call_target="tpu_custom_call" | custom-call | flops 1000000000 | bytes 4194304 | tf_op jit(solution)/shard_map/galerkin/pallas_call | solution.py:506
  41.4 1.1 %copy.7 = f32[64,5120]{1,0:T(8,128)} copy(f32[64,5120]{1,0:T(8,128)S(1)} %galerkin.1) | data formatting | bytes 2621440

commit v6 on v5

--- a/solution.py
+++ b/solution.py
@@ -372,17 +372,16 @@
     def passed_on(side, turn):
         return [(2 * order[turn] + 1, turn)] if side == 0 else [(2 * order[turn] + n, n) for n in range(2 - 2 * min(turn, 1))]
 
-    def pass_on(turn):
-        for side in range(2):
-            if far and passed_on(side, turn):
-
-                @pl.when(is_passer[side])
-                def _():
-                    if side:
-                        pl.semaphore_wait(ready.at[4], 1)
-                    for step, index in passed_on(side, turn):
-                        pass_copy(side, step, index).wait_recv()
-                        on_copy(side, step, index).start()
+    def pass_on(side, turn):
+        if far:
+
+            @pl.when(is_passer[side])
+            def _():
+                if side:
+                    pl.semaphore_wait(ready.at[4], 1)
+                for step, index in passed_on(side, turn):
+                    pass_copy(side, step, index).wait_recv()
+                    on_copy(side, step, index).start()
 
     def finish(step):
         halo_copy(step, 0).wait_recv()
@@ -427,6 +426,12 @@
     def _():
         y_take(3)
 
+    if far:
+
+        @pl.when(is_last)
+        def _():
+            signal(ready.at[2], (blk, below))
+
     x_take(0)
 
     @pl.when(jnp.logical_not(is_last))
@@ -442,12 +447,6 @@
     @pl.when(is_end)
     def _():
         y_take(3)
-
-    if far:
-
-        @pl.when(is_last)
-        def _():
-            signal(ready.at[2], (blk, below))
 
     serve(3)
     x_take(1)
@@ -457,15 +456,16 @@
         def _():
             pl.semaphore_wait(ready.at[1], 1)
 
+    pass_on(0, 0)
     multiply(1)
-    pass_on(0)
+    pass_on(1, 0)
     x_take(2)
+    pass_on(0, 1)
     multiply(2)
-    pass_on(1)
+    pass_on(0, 2)
     x_take(3)
+    pass_on(0, 3)
     multiply(3)
-    pass_on(2)
-    pass_on(3)
     for turn in range(4):
         both_steps(turn, finish)
 

time: 42.8 us -> 41.4 us (0.967)
  Pallas kernels: 41.4 us -> 40.2 us
    pallas_call x1, Pallas kernels: 41.4 us -> 40.2 us  [body(): pl.pallas_call(kernel, out_shape=jax.ShapeDtypeStruct((B, 5 * NX * NY * B...]
where the time goes in v6:
time: 41.4 us; the launch traced here: 41.2 us
  Pallas kernels  40.2 us (97%)
  local copies, waits for them, and re-layouts  1.06 us (3%)
    pallas_call x1, Pallas kernels, body(): pl.pallas_call(kernel, out_shape=jax.ShapeDtypeStruct((B, 5 * NX * NY * B...  40.2 us
    unnamed x1, local copies, waits for them, and re-layouts  1.06 us

profile of v6, /device:TPU:6, one launch (start us, length us, event | category | flops | bytes accessed | tf_op | source)
XLA Modules:
  0.0 41.2 jit_solution(14720352567672756079)
XLA Ops:
  0.0 40.2 %galerkin.1 = f32[64,5120]{1,0:T(8,128)S(1)} custom-call(f32[4,64,256]{2,1,0:T(8,128)} %a_hbm.1, f32[256,128]{1,0:T(8,128)} %bitcast.2, s32[4,4]{1,0:T(4,128)} %group_hbm.1, s32[4,4]{1,0:T(4,128)} %row_hbm.1, s32[2,4]{1,0:T(2,128)} %bitcast.3), custom_call_target="tpu_custom_call" | custom-call | flops 1000000000 | bytes 4194304 | tf_op jit(solution)/shard_map/galerkin/pallas_call | solution.py:506
  40.2 1.1 %copy.7 = f32[64,5120]{1,0:T(8,128)} copy(f32[64,5120]{1,0:T(8,128)S(1)} %galerkin.1) | data formatting | bytes 2621440

commit v7 on v6

--- a/solution.py
+++ b/solution.py
@@ -351,7 +351,7 @@
 
     def detour(side, turn, n):
         if side == 0:
-            return is_last & (n == 1), turn
+            return is_last & (n == 0), turn
         return is_first & (turn == 0), n
 
     def each_way(side, turn, n, act):
@@ -370,7 +370,7 @@
             act(halo_copy(step, side))
 
     def passed_on(side, turn):
-        return [(2 * order[turn] + 1, turn)] if side == 0 else [(2 * order[turn] + n, n) for n in range(2 - 2 * min(turn, 1))]
+        return [(2 * order[turn], turn)] if side == 0 else [(2 * order[turn] + n, n) for n in range(2 - 2 * min(turn, 1))]
 
     def pass_on(side, turn):
         if far:
@@ -463,8 +463,8 @@
     pass_on(0, 1)
     multiply(2)
     pass_on(0, 2)
+    pass_on(0, 3)
     x_take(3)
-    pass_on(0, 3)
     multiply(3)
     for turn in range(4):
         both_steps(turn, finish)

time: 41.4 us -> 41.3 us (level)
  no operation moved by 1% of the time
where the time goes in v7:
time: 41.3 us; the launch traced here: 41.2 us
  Pallas kernels  40.1 us (97%)
  local copies, waits for them, and re-layouts  1.06 us (3%)
    pallas_call x1, Pallas kernels, body(): pl.pallas_call(kernel, out_shape=jax.ShapeDtypeStruct((B, 5 * NX * NY * B...  40.1 us
    unnamed x1, local copies, waits for them, and re-layouts  1.06 us

profile of v7, /device:TPU:6, one launch (start us, length us, event | category | flops | bytes accessed | tf_op | source)
XLA Modules:
  0.0 41.2 jit_solution(14713011925082792921)
XLA Ops:
  0.0 40.1 %galerkin.1 = f32[64,5120]{1,0:T(8,128)S(1)} custom-call(f32[4,64,256]{2,1,0:T(8,128)} %a_hbm.1, f32[256,128]{1,0:T(8,128)} %bitcast.2, s32[4,4]{1,0:T(4,128)} %group_hbm.1, s32[4,4]{1,0:T(4,128)} %row_hbm.1, s32[2,4]{1,0:T(2,128)} %bitcast.3), custom_call_target="tpu_custom_call" | custom-call | flops 1000000000 | bytes 4194304 | tf_op jit(solution)/shard_map/galerkin/pallas_call | solution.py:506
  40.1 1.1 %copy.7 = f32[64,5120]{1,0:T(8,128)} copy(f32[64,5120]{1,0:T(8,128)S(1)} %galerkin.1) | data formatting | bytes 2621440

commit v8 on v7

--- a/solution.py
+++ b/solution.py
@@ -415,10 +415,8 @@
     for shift in range(1, NX):
         ask_landing(shift).wait_recv()
     serve(0)
-    lax.fori_loop(2, 3, left_product, 0)
     y_take(1)
     serve(1)
-    lax.fori_loop(3, 4, left_product, 0)
     y_take(2)
     serve(2)
 
@@ -432,6 +430,7 @@
         def _():
             signal(ready.at[2], (blk, below))
 
+    lax.fori_loop(2, FB, left_product, 0)
     x_take(0)
 
     @pl.when(jnp.logical_not(is_last))

time: 41.3 us -> 41 us (level); the launches traced: 41.2 us -> 40.5 us
  Pallas kernels: 40.1 us -> 39.4 us
    pallas_call x1, Pallas kernels: 40.1 us -> 39.4 us  [body(): pl.pallas_call(kernel, out_shape=jax.ShapeDtypeStruct((B, 5 * NX * NY * B...]
where the time goes in v8:
time: 41 us; the launch traced here: 40.5 us
  Pallas kernels  39.4 us (96%)
  local copies, waits for them, and re-layouts  1.06 us (3%)
    pallas_call x1, Pallas kernels, body(): pl.pallas_call(kernel, out_shape=jax.ShapeDtypeStruct((B, 5 * NX * NY * B...  39.4 us
    unnamed x1, local copies, waits for them, and re-layouts  1.06 us

profile of v8, /device:TPU:6, one launch (start us, length us, event | category | flops | bytes accessed | tf_op | source)
XLA Modules:
  0.0 40.5 jit_solution(3453968303407331973)
XLA Ops:
  0.0 39.4 %galerkin.1 = f32[64,5120]{1,0:T(8,128)S(1)} custom-call(f32[4,64,256]{2,1,0:T(8,128)} %a_hbm.1, f32[256,128]{1,0:T(8,128)} %bitcast.2, s32[4,4]{1,0:T(4,128)} %group_hbm.1, s32[4,4]{1,0:T(4,128)} %row_hbm.1, s32[2,4]{1,0:T(2,128)} %bitcast.3), custom_call_target="tpu_custom_call" | custom-call | flops 1000000000 | bytes 4194304 | tf_op jit(solution)/shard_map/galerkin/pallas_call | solution.py:505
  39.4 1.1 %copy.7 = f32[64,5120]{1,0:T(8,128)} copy(f32[64,5120]{1,0:T(8,128)S(1)} %galerkin.1) | data formatting | bytes 2621440

commit v9 on v8

--- a/solution.py
+++ b/solution.py
@@ -245,9 +245,13 @@
             def _():
                 hand_on(part).start()
 
-    def x_take(turn):
-        for shift in range(1, NX):
-            x_landing(order[turn], shift).wait_recv()
+    def x_take(turn, n):
+        for column in (2 * n, 2 * n + 1):
+            shift = (x + NX - column) % NX
+
+            @pl.when(shift != 0)
+            def _():
+                x_landing(order[turn], shift).wait_recv()
 
     @pl.when(jnp.logical_not(is_first))
     def _():
@@ -403,6 +407,7 @@
 
     def multiply(turn):
         def one(n, carry):
+            x_take(turn, n)
             compute(2 * order[turn] + n)
             for side in range(2):
                 each_way(side, turn, n, lambda copy: copy.start())
@@ -431,7 +436,6 @@
             signal(ready.at[2], (blk, below))
 
     lax.fori_loop(2, FB, left_product, 0)
-    x_take(0)
 
     @pl.when(jnp.logical_not(is_last))
     def _():
@@ -448,7 +452,6 @@
         y_take(3)
 
     serve(3)
-    x_take(1)
     if far:
 
         @pl.when(is_first)
@@ -458,12 +461,10 @@
     pass_on(0, 0)
     multiply(1)
     pass_on(1, 0)
-    x_take(2)
     pass_on(0, 1)
     multiply(2)
     pass_on(0, 2)
     pass_on(0, 3)
-    x_take(3)
     multiply(3)
     for turn in range(4):
         both_steps(turn, finish)

time: 41 us -> 41.3 us (level)
  no operation moved by 1% of the time
where the time goes in v9:
time: 41.3 us; the launch traced here: 40.7 us
  Pallas kernels  39.6 us (96%)
  local copies, waits for them, and re-layouts  1.06 us (3%)
    pallas_call x1, Pallas kernels, body(): pl.pallas_call(kernel, out_shape=jax.ShapeDtypeStruct((B, 5 * NX * NY * B...  39.6 us
    unnamed x1, local copies, waits for them, and re-layouts  1.06 us

profile of v9, /device:TPU:6, one launch (start us, length us, event | category | flops | bytes accessed | tf_op | source)
XLA Modules:
  0.0 40.7 jit_solution(3176089099641250634)
XLA Ops:
  0.0 39.6 %galerkin.1 = f32[64,5120]{1,0:T(8,128)S(1)} custom-call(f32[4,64,256]{2,1,0:T(8,128)} %a_hbm.1, f32[256,128]{1,0:T(8,128)} %bitcast.2, s32[4,4]{1,0:T(4,128)} %group_hbm.1, s32[4,4]{1,0:T(4,128)} %row_hbm.1, s32[2,4]{1,0:T(2,128)} %bitcast.3), custom_call_target="tpu_custom_call" | custom-call | flops 1000000000 | bytes 4194304 | tf_op jit(solution)/shard_map/galerkin/pallas_call | solution.py:506
  39.7 1.1 %copy.7 = f32[64,5120]{1,0:T(8,128)} copy(f32[64,5120]{1,0:T(8,128)S(1)} %galerkin.1) | data formatting | bytes 2621440
